TPU v7x, 32 devices: a whole 2x2x4 slice. The times are simulated.
32 devices in a mesh: grp: 2 (over x), rcv: 16 (over z, y, core).
Axes of the slice: x: 2, y: 2, z: 4, core: 2. Of those that a mesh axis runs over, the one named last changes fastest.
Arguments:
- records: bfloat16 [8, 1024, 2048], P('grp', 'rcv'), parts along dimension 0, may hold values from -40 to 40, as said below
- quality: int32 [8, 1024], P('grp', 'rcv'), parts along dimension 0, may hold values 0 or 1
- block_ids: int32 [4], P('grp'), parts along dimension 0, may hold values from 0 to 15, as said below
Outputs:
- stacked: bfloat16 [16, 64, 128, 1024], P('rcv', 'grp'), parts along dimension 1
There are 2 independent parts, one for each index of `grp`. A program takes and returns all parts, laid end to end along the dimension named above; each array names one. Nothing has to cross between parts.
Inputs may be any that keep to these rules, and one draw needn't show every extreme that they name: records hold finite samples. `block_ids`: 2 distinct block numbers.
All inputs are finite; a program needn't handle non-finite values. No bound on the sum of `quality` on one device may be relied on, other than what follows from the above.
Results may differ from a plain program's by a relative error of at most 0.0066.
Values may be sent and summed in bfloat16 or wider, within the bound.
A program may use at most 64 MiB of HBM per device.

v0:
```python
import jax
import jax.numpy as jnp
from jax import lax
from jax.sharding import PartitionSpec as P

NB = 8
BIN = 32
FLO = 64
SBLK = 64
NSB = 2


def from_partner(value, axis, stride):
    mask = 2**stride
    pairs = [(source, source ^ mask) for source in range(lax.axis_size(axis))]
    return lax.ppermute(value, axis, pairs)


def make_basis(samples):
    times = jnp.arange(samples, dtype=jnp.int32)
    bins_all = FLO + jnp.arange(NB * BIN, dtype=jnp.int32)
    phases = times[:, None] * bins_all[None, :] % samples
    angles = phases.astype(jnp.float32) * (2.0 * jnp.pi / samples)
    cosine = jnp.cos(angles).reshape(samples, NB, 1, BIN)
    sine_neg = (-jnp.sin(angles)).reshape(samples, NB, 1, BIN)
    return (
        jnp.concatenate([cosine, sine_neg], axis=2)
        .reshape(samples, NB * 2 * BIN)
        .astype(jnp.bfloat16)
    )


def per_device(records, quality, block_ids):
    devices = lax.axis_size("rcv")
    groups = devices // NB
    windows, channels, samples = records.shape
    sub_rows = channels // groups
    basis_table = make_basis(samples).reshape(samples, NB, 2 * BIN)
    rec_rows = records.reshape(windows, groups, sub_rows, samples)
    spectrum = jnp.einsum(
        "wqjs,sbm->bqwjm", rec_rows, basis_table, preferred_element_type=jnp.float32
    )
    band_power = jnp.sum(spectrum * spectrum, axis=-1) / BIN
    keep_gate = quality.reshape(windows, groups, sub_rows).transpose(1, 0, 2).astype(jnp.float32)
    scaling = keep_gate[None] * lax.rsqrt(band_power + 1e-05)
    whitened = (spectrum * scaling[..., None]).astype(jnp.bfloat16)
    send_buf = whitened.reshape(devices, windows, sub_rows * 2 * BIN)
    arrived = lax.all_to_all(send_buf, "rcv", split_axis=0, concat_axis=0, tiled=True)
    receivers = arrived.reshape(devices, windows, sub_rows, 2, BIN)
    my_index = lax.axis_index("rcv")
    per_block = channels // SBLK
    blk_rows = SBLK // sub_rows
    own_pieces = []
    for source_slot in range(NSB):
        owner_dev = block_ids[source_slot] // per_block
        own_pieces.append(lax.dynamic_index_in_dim(arrived, owner_dev, 0, keepdims=False))
    collected = jnp.stack(own_pieces)[None]
    my_group = my_index % groups
    for bit_level in range(groups.bit_length() - 1):
        partner = from_partner(collected, "rcv", bit_level)
        upper_side = my_group // 2**bit_level % 2 == 1
        low_half = jnp.where(upper_side, partner, collected)
        high_half = jnp.where(upper_side, collected, partner)
        collected = jnp.concatenate([low_half, high_half], axis=0)
    slices = []
    for source_slot in range(NSB):
        first_group = block_ids[source_slot] % per_block * blk_rows
        slices.append(collected[:, source_slot])
    src_band = jnp.stack(slices).reshape(NSB, blk_rows, windows, sub_rows, 2, BIN)
    source_count = NSB * SBLK
    group_width = devices * sub_rows
    left_side = src_band.transpose(5, 0, 1, 3, 2, 4).reshape(BIN, source_count, windows, 2)
    rec_cols = receivers.transpose(4, 1, 3, 0, 2).reshape(BIN, windows, 2, group_width)
    rotated = jnp.stack([rec_cols[:, :, 1], -rec_cols[:, :, 0]], axis=2)
    right_side = jnp.concatenate([rec_cols, rotated], axis=-1)
    joined = jnp.einsum("inwp,iwpk->ink", left_side, right_side, preferred_element_type=jnp.float32)
    return (joined * (1.0 / windows)).astype(jnp.bfloat16)[None]


def solution(mesh):
    placed = (P("grp", "rcv", None), P("grp", "rcv"), P("grp"))
    return jax.shard_map(
        per_device,
        mesh=mesh,
        in_specs=placed,
        out_specs=P("rcv", "grp", None, None),
        check_vma=False,
    )
```

profile of v0, /device:TPU:0, one launch (start us, length us, event | category | flops | bytes accessed | tf_op | source)
XLA Modules:
  0.0 40.0 jit_solution(10602130683415514435)
XLA Ops:
  0.0 0.0 copy-start
  0.0 0.8 %convert_element_type.44 = f32[4,64]{1,0:T(4,128)S(1)} convert(s32[4,64]{1,0:T(4,128)} %param.4) | non-fusion elementwise | flops 256 | bytes 2048 | tf_op jit(solution)/shard_map/convert_element_type | solution.py:44
  0.8 0.1 convert_element_type.45
  0.9 9.0 %cosine_convert_fusion = (bf16[2048,8,1,32]{0,3,2,1:T(8,128)(2,1)S(1)}, bf16[2048,8,1,32]{0,3,2,1:T(8,128)(2,1)S(1)}) fusion(s32[8,32]{1,0:T(8,128)S(1)} %add_add_fusion), kind=kLoop, calls=%fused_computation.11 | loop fusion | flops 8912896 | bytes 2098176 | tf_op jit(solution)/shard_map/convert
  9.8 0.2 pad_maximum_fusion
  10.0 0.0 copy-done
  10.1 1.5 %multiply_reduce_fusion = (f32[8,2,4,32]{3,1,2,0:T(2,128)S(1)}, f32[8,2,4,32,64]{4,3,1,2,0:T(8,128)S(1)}) fusion(bf16[2048,8,64,1,1]{0,2,4,3,1:T(8,128)(2,1)S(1)} %bitcast.44, bf16[4,2,32,2048,1]{3,2,1,0,4:T(8,128)(2,1)S(1)} %bitcast.42), kind=kOutput, calls=%fused_computation.17 | convolution fusion | flops 537131008 | bytes 3678208 | tf_op jit(solution)/shard_map/wqjs,sbm->bqwjm/dot_general | solution.py:40
  11.5 0.0 copy-start.1
  11.6 0.3 multiply_convert_fusion
  11.9 0.1 copy.14
  12.0 1.1 %reshape.128 = bf16[16,4,2048]{2,1,0:T(4,128)(2,1)} reshape(bf16[8,2,4,32,64]{4,3,2,1,0:T(8,128)(2,1)S(1)} %copy.14) | data formatting | bytes 524288 | tf_op jit(solution)/shard_map/reshape | solution.py:47
  13.1 7.4 %all-to-all-start = ((bf16[16,4,2048]{2,1,0:T(4,128)(2,1)}), bf16[16,4,2048]{2,1,0:T(4,128)(2,1)S(1)}, u32[]{:S(2)}, u32[]{:S(2)}) async-start(bf16[16,4,2048]{2,1,0:T(4,128)(2,1)} %reshape.128), calls=%async_computation | async-start | bytes 524288 | tf_op jit(solution)/shard_map/all_to_all | solution.py:48
  20.5 0.0 copy-done.1
  20.5 0.6 %fusion.16 = (s32[1]{0:T(128)}, s32[1]{0:T(128)}) fusion(s32[2]{0:T(128)S(1)} %copy-done.1), kind=kLoop, calls=%fused_computation.38 | loop fusion | bytes 16 | tf_op jit(solution)/shard_map/slice | solution.py:55
  24.9 5.6 %all-to-all-done = bf16[16,4,2048]{2,1,0:T(4,128)(2,1)S(1)} async-done(((bf16[16,4,2048]{2,1,0:T(4,128)(2,1)}), bf16[16,4,2048]{2,1,0:T(4,128)(2,1)S(1)}, u32[]{:S(2)}, u32[]{:S(2)}) %all-to-all-start) | async-done | bytes 262176 | tf_op jit(solution)/shard_map/all_to_all | solution.py:48
  30.5 0.1 collective-permute-start
  30.6 0.2 copy.10
  30.8 0.8 %reshape.123 = bf16[16,4,32,2,32]{4,3,2,0,1:T(2,128)(2,1)S(1)} reshape(bf16[16,4,2048]{2,0,1:T(8,128)(2,1)S(1)} %copy.10) | data formatting | bytes 524288 | tf_op jit(solution)/shard_map/reshape | solution.py:49
  31.6 0.8 %copy.15 = bf16[32,4,2,512]{3,1,2,0:T(4,128)(2,1)S(1)} copy(bf16[32,4,2,512]{0,2,3,1:T(2,128)(2,1)S(1)} %bitcast.43) | data formatting | bytes 524288 | tf_op jit(solution)/shard_map/reshape | solution.py:73
  32.4 0.1 fusion.15
  32.5 0.0 collective-permute-done
  32.7 0.1 stack.17
  32.8 0.1 stack.18
  33.0 0.4 %maximum_bitcast_fusion = bf16[32,2,2,32,4,2]{0,5,3,4,2,1:T(2,128)(2,1)S(1)} fusion(bf16[1,2,4,32,2,32]{5,4,3,2,1,0:T(2,128)(2,1)S(1)} %stack.18, bf16[1,2,4,32,2,32]{5,4,3,2,1,0:T(2,128)(2,1)S(1)} %stack.17), kind=kLoop, calls=%fused_computation.23 | loop fusion | flops 32768 | bytes 131072 | tf_op jit(solution)/shard_map/transpose | solution.py:72
  33.4 0.5 %copy.9 = bf16[32,2,2,32,4,2]{3,2,1,4,5,0:T(2,128)(2,1)S(1)} copy(bf16[32,2,2,32,4,2]{0,5,3,4,2,1:T(2,128)(2,1)S(1)} %maximum_bitcast_fusion) | data formatting | bytes 131072 | tf_op jit(solution)/shard_map/transpose | solution.py:72
  33.9 0.2 reshape.122
  34.0 6.0 %fusion.1 = bf16[1,32,128,1024]{3,2,1,0:T(8,128)(2,1)} fusion(bf16[32,128,4,2]{1,2,3,0:T(4,128)(2,1)S(1)} %reshape.122, bf16[32,4,1,512]{3,1,2,0:T(4,128)(2,1)S(1)} %get-tuple-element.6, bf16[32,4,1,512]{3,1,2,0:T(4,128)(2,1)S(1)} %get-tuple-element.5, bf16[32,4,2,512]{3,1,2,0:T(4,128)(2,1)S(1)} %copy.15), kind=kOutput, calls=%fused_computation.2 | convolution fusion | flops 77070336 | bytes 8978432 | tf_op jit(solution)/shard_map/inwp,iwpk->ink/dot_general | solution.py:76
  (6 shorter events, 0.2 us)
Async XLA Ops:
  0.0 10.0 %copy-start = (bf16[4,64,2048]{2,1,0:T(8,128)(2,1)S(1)}, bf16[4,64,2048]{2,1,0:T(8,128)(2,1)}, u32[]{:S(2)}) copy-start(bf16[4,64,2048]{2,1,0:T(8,128)(2,1)} %param.3) | copy-start | bytes 3145732
  11.5 9.0 %copy-start.1 = (s32[2]{0:T(128)S(1)}, s32[2]{0:T(128)}, u32[]{:S(2)}) copy-start(s32[2]{0:T(128)} %param.5) | copy-start | bytes 28
  13.1 17.4 %all-to-all-start = ((bf16[16,4,2048]{2,1,0:T(4,128)(2,1)}), bf16[16,4,2048]{2,1,0:T(4,128)(2,1)S(1)}, u32[]{:S(2)}, u32[]{:S(2)}) async-start(bf16[16,4,2048]{2,1,0:T(4,128)(2,1)} %reshape.128), calls=%async_computation | async-start | bytes 524288 | tf_op jit(solution)/shard_map/all_to_all | solution.py:48
  30.5 2.0 %collective-permute-start = (bf16[1,2,4,2048]{3,2,1,0:T(4,128)(2,1)S(1)}, bf16[1,2,4,2048]{3,2,1,0:T(4,128)(2,1)S(1)}, u32[]{:S(2)}, u32[]{:S(2)}) collective-permute-start(bf16[1,2,4,2048]{3,2,1,0:T(4,128)(2,1)S(1)} %maximum_bitcast_fusion.1), channel_id=1, source_target_pairs={{0,1},{1,0},{2,3},{3,2},{4,5},{5,4},{6,7},{7,6},{8,9},{9,8},{10,11... | collective-permute-start | bytes 98312 | tf_op jit(solution)/shard_map/ppermute | solution.py:16
where the time goes:
time: 40.4 us; the launch traced here: 40 us
  other arithmetic  11 us (27%)
  starting transfers between devices  7.46 us (18%)
  matrix products  7.45 us (18%)
  waiting for transfers between devices  5.62 us (14%)
  local copies, waits for them, and re-layouts  4.52 us (11%)
  between operations  4 us (10%)
    another operation x1, other arithmetic  8.96 us
    all_to_all x1, starting transfers between devices, per_device(): lax.all_to_all(send_buf, 'rcv', split_axis=0, concat_axis=0, tiled=True)  7.39 us
    dot_general x1, matrix products, per_device(): jnp.einsum('inwp,iwpk->ink', left_side, right_side, preferred_element_typ...  5.99 us
    all_to_all x1, waiting for transfers between devices, per_device(): lax.all_to_all(send_buf, 'rcv', split_axis=0, concat_axis=0, tiled=True)  5.61 us
    dot_general x1, matrix products, per_device(): jnp.einsum('wqjs,sbm->bqwjm', rec_rows, basis_table, preferred_element_ty...  1.46 us
    reshape x2, local copies, waits for them, and re-layouts, per_device(): send_buf = whitened.reshape(devices, windows, sub_rows * 2 * BIN)  1.13 us
    reshape x1, local copies, waits for them, and re-layouts, per_device(): receivers.transpose(4, 1, 3, 0, 2).reshape(BIN, windows, 2, group_width)  0.83 us
  transfers between devices with their start and end apart: 2, of which 1 were waited for; matrix products, arithmetic and copies ran while one was open for 6% of the time, Pallas kernels for 0%

commit v1 on v0

--- a/solution.py
+++ b/solution.py
@@ -1,6 +1,12 @@
+import functools
+
 import jax
 import jax.numpy as jnp
+import ml_dtypes
+import numpy as np
 from jax import lax
+from jax.experimental import pallas as pl
+from jax.experimental.pallas import tpu as pltpu
 from jax.sharding import PartitionSpec as P
 
 NB = 8
@@ -8,6 +14,250 @@
 FLO = 64
 SBLK = 64
 NSB = 2
+LANES = 128
+
+
+def basis_rows(samples, count):
+    times = np.arange(count, dtype=np.int64)
+    bins = FLO + np.arange(NB * BIN, dtype=np.int64)
+    phases = (bins[:, None] * times[None, :]) % samples
+    angles = phases.astype(np.float64) * (2.0 * np.pi / samples)
+    table = np.stack([np.cos(angles), -np.sin(angles)]).reshape(2, NB, BIN, count)
+    table = table.transpose(1, 0, 2, 3).reshape(NB * 2 * BIN, count)
+    return table.astype(np.float32).astype(ml_dtypes.bfloat16)
+
+
+def lanes_to_rows(pieces, width):
+    lane = lax.broadcasted_iota(jnp.int32, pieces[0].shape, 1) // width
+    wide = [piece.astype(jnp.float32) for piece in pieces]
+    result = []
+    for w in range(len(pieces)):
+        total = None
+        for e, piece in enumerate(wide):
+            shift = (e - w) * width % LANES
+            moved = pltpu.roll(piece, shift, 1) if shift else piece
+            total = moved if total is None else jnp.where(lane == e, moved, total)
+        result.append(total)
+    return result
+
+
+def flipped(me, off):
+    other, bit = me, 1
+    while bit <= off:
+        if off & bit:
+            other = other + bit * (1 - 2 * (me // bit % 2))
+        bit *= 2
+    return other
+
+
+def exchange_kernel(
+    ids_ref, quality_ref, basis_ref, records_ref, rhs_ref, src_ref,
+    basis_v, rec_v, send_v, recv_v, rhs_v, own_v,
+    load_sem, send_sem, recv_sem, plane_sem, src_sem,
+):
+    devices = recv_v.shape[0]
+    windows, channels, samples = records_ref.shape
+    groups = devices // NB
+    sub_rows = channels // groups
+    pack = LANES // sub_rows
+    planes = devices // pack
+    half = samples // 2
+    rows = 2 * BIN
+    me = lax.axis_index("rcv")
+
+    loads = [pltpu.make_async_copy(basis_ref, basis_v, load_sem.at[0])]
+    for q in range(groups):
+        for w in range(windows):
+            place = q * windows + w
+            loads.append(
+                pltpu.make_async_copy(
+                    records_ref.at[w, pl.ds(q * sub_rows, sub_rows)],
+                    rec_v.at[pl.ds(place * sub_rows, sub_rows)],
+                    load_sem.at[1 + place],
+                )
+            )
+    for load in loads:
+        load.start()
+
+    barrier = pltpu.get_barrier_semaphore()
+    for off in range(1, devices):
+        pl.semaphore_signal(
+            barrier, inc=1, device_id={"rcv": flipped(me, off)},
+            device_id_type=pl.DeviceIdType.MESH,
+        )
+
+    keep = jnp.concatenate(
+        [
+            quality_ref[w : w + 1, q * sub_rows : (q + 1) * sub_rows]
+            for q in range(groups)
+            for w in range(windows)
+        ],
+        axis=1,
+    ).astype(jnp.float32)
+    for load in loads:
+        load.wait()
+
+    contract = (((1,), (1,)), ((), ()))
+    low = lax.dot_general(
+        basis_v[...], rec_v[:, :half], contract, preferred_element_type=jnp.float32
+    )
+    high = lax.dot_general(
+        basis_v[...], rec_v[:, half:], contract, preferred_element_type=jnp.float32
+    )
+    odd = lax.broadcasted_iota(jnp.int32, (rows, low.shape[1]), 0) % 2 == 1
+    for b in range(NB):
+        band = slice(b * rows, (b + 1) * rows)
+        spectrum = low[band] + jnp.where(odd, -high[band], high[band])
+        power = jnp.sum(spectrum * spectrum, axis=0, keepdims=True) / BIN
+        white = (spectrum * (keep * lax.rsqrt(power + 1e-05))).astype(jnp.bfloat16)
+        for q in range(groups):
+            send_v[b * groups + q] = white[:, q * LANES : (q + 1) * LANES]
+
+    pl.semaphore_wait(barrier, devices - 1)
+    copies = {}
+    for off in range(devices - 1, 0, -1):
+        peer = flipped(me, off)
+        copies[off] = pltpu.make_async_remote_copy(
+            src_ref=send_v.at[peer], dst_ref=recv_v.at[me],
+            send_sem=send_sem.at[off], recv_sem=recv_sem.at[off],
+            device_id={"rcv": peer}, device_id_type=pl.DeviceIdType.MESH,
+        )
+        copies[off].start()
+    recv_v[me] = send_v[me]
+
+    outs = []
+    for dz in range(planes):
+        plane = flipped(me // pack, dz)
+        for e in range(pack):
+            off = dz * pack + e
+            if off:
+                copies[off].wait_recv()
+        if dz == planes - 1:
+            for s in range(NSB):
+                own_v[s] = recv_v[ids_ref[s]]
+            swap = pltpu.make_async_remote_copy(
+                src_ref=own_v, dst_ref=src_ref.at[me % groups],
+                send_sem=src_sem.at[0], recv_sem=src_sem.at[1],
+                device_id={"rcv": flipped(me, 1)}, device_id_type=pl.DeviceIdType.MESH,
+            )
+            swap.start()
+            keep_own = pltpu.make_async_copy(own_v, src_ref.at[me % groups], src_sem.at[2])
+            keep_own.start()
+        by_window = lanes_to_rows([recv_v[plane * pack + e] for e in range(pack)], sub_rows)
+        for w, block in enumerate(by_window):
+            real, imag = block[:BIN], block[BIN:]
+            rhs_v[0, plane, w * rows : w * rows + BIN] = real.astype(jnp.bfloat16)
+            rhs_v[0, plane, w * rows + BIN : (w + 1) * rows] = imag.astype(jnp.bfloat16)
+            rhs_v[1, plane, w * rows : w * rows + BIN] = imag.astype(jnp.bfloat16)
+            rhs_v[1, plane, w * rows + BIN : (w + 1) * rows] = (-real).astype(jnp.bfloat16)
+        for part in range(2):
+            out = pltpu.make_async_copy(
+                rhs_v.at[part, plane], rhs_ref.at[part, plane], plane_sem.at[part, dz]
+            )
+            out.start()
+            outs.append(out)
+    for off in range(devices - 1, 0, -1):
+        copies[off].wait_send()
+    for out in outs:
+        out.wait()
+    keep_own.wait()
+    swap.wait()
+
+
+def product_kernel(src_ref, rhs_ref, out_ref, left_v):
+    step = pl.program_id(0)
+    bins = out_ref.shape[0]
+    rows = 2 * BIN
+    windows = rhs_ref.shape[2] // rows
+    groups, blocks = src_ref.shape[:2]
+    sub_rows = SBLK // groups
+
+    @pl.when(step == 0)
+    def _():
+        pieces = [src_ref[q, s] for s in range(blocks) for q in range(groups)]
+        by_window = lanes_to_rows(pieces, sub_rows)
+        left_v[...] = jnp.concatenate(by_window, axis=0).T * (1.0 / windows)
+
+    left = left_v[...]
+    bin_of = lax.broadcasted_iota(jnp.int32, left.shape, 1) % BIN
+    masked = jnp.concatenate(
+        [jnp.where(bin_of == step * bins + i, left, 0.0).astype(jnp.bfloat16) for i in range(bins)],
+        axis=0,
+    )
+    planes = rhs_ref.shape[1]
+    wide = 2
+    for part in range(2):
+        for z in range(0, planes, wide):
+            right = jnp.concatenate([rhs_ref[part, z + u] for u in range(wide)], axis=1)
+            both = jnp.dot(masked, right, preferred_element_type=jnp.float32)
+            first = (part * planes + z) * LANES
+            out_ref[:, :, first : first + wide * LANES] = both.astype(jnp.bfloat16).reshape(
+                bins, left.shape[0], wide * LANES
+            )
+
+
+def per_device_kernels(records, quality, block_ids):
+    devices = lax.axis_size("rcv")
+    groups = devices // NB
+    windows, channels, samples = records.shape
+    sub_rows = channels // groups
+    pack = LANES // sub_rows
+    planes = devices // pack
+    rows = 2 * BIN
+    depth = windows * rows
+    basis = jnp.asarray(basis_rows(samples, samples // 2))
+    rhs, src = pl.pallas_call(
+        exchange_kernel,
+        out_shape=(
+            jax.ShapeDtypeStruct((2, planes, depth, LANES), jnp.bfloat16),
+            jax.ShapeDtypeStruct((groups, NSB, rows, LANES), jnp.bfloat16),
+        ),
+        in_specs=[
+            pl.BlockSpec(memory_space=pltpu.SMEM),
+            pl.BlockSpec(memory_space=pltpu.VMEM),
+            pl.BlockSpec(memory_space=pl.ANY),
+            pl.BlockSpec(memory_space=pl.ANY),
+        ],
+        out_specs=(pl.BlockSpec(memory_space=pl.ANY), pl.BlockSpec(memory_space=pl.ANY)),
+        scratch_shapes=[
+            pltpu.VMEM(basis.shape, jnp.bfloat16),
+            pltpu.VMEM((windows * channels, samples), jnp.bfloat16),
+            pltpu.VMEM((devices, rows, LANES), jnp.bfloat16),
+            pltpu.VMEM((devices, rows, LANES), jnp.bfloat16),
+            pltpu.VMEM((2, planes, depth, LANES), jnp.bfloat16),
+            pltpu.VMEM((NSB, rows, LANES), jnp.bfloat16),
+            pltpu.SemaphoreType.DMA((1 + groups * windows,)),
+            pltpu.SemaphoreType.DMA((devices,)),
+            pltpu.SemaphoreType.DMA((devices,)),
+            pltpu.SemaphoreType.DMA((2, planes)),
+            pltpu.SemaphoreType.DMA((3,)),
+        ],
+        compiler_params=pltpu.CompilerParams(
+            collective_id=0, has_side_effects=True, vmem_limit_bytes=32 * 2**20
+        ),
+        name="spectra_exchange",
+    )(block_ids, quality, basis, records)
+
+    count = NSB * SBLK
+    step_bins = 4
+    joined = pl.pallas_call(
+        product_kernel,
+        grid=(BIN // step_bins,),
+        out_shape=jax.ShapeDtypeStruct((BIN, count, 2 * planes * LANES), jnp.bfloat16),
+        in_specs=[
+            pl.BlockSpec(src.shape, lambda i: (0, 0, 0, 0)),
+            pl.BlockSpec(rhs.shape, lambda i: (0, 0, 0, 0)),
+        ],
+        out_specs=pl.BlockSpec((step_bins, count, 2 * planes * LANES), lambda i: (i, 0, 0)),
+        scratch_shapes=[pltpu.VMEM((count, depth), jnp.float32)],
+        compiler_params=pltpu.CompilerParams(vmem_limit_bytes=32 * 2**20),
+        name="cross_spectra",
+    )(src, rhs)
+    return joined[None]
+
+
+def make_basis(samples):
+    return jnp.asarray(basis_rows(samples, samples).T)
 
 
 def from_partner(value, axis, stride):
@@ -16,21 +266,7 @@
     return lax.ppermute(value, axis, pairs)
 
 
-def make_basis(samples):
-    times = jnp.arange(samples, dtype=jnp.int32)
-    bins_all = FLO + jnp.arange(NB * BIN, dtype=jnp.int32)
-    phases = times[:, None] * bins_all[None, :] % samples
-    angles = phases.astype(jnp.float32) * (2.0 * jnp.pi / samples)
-    cosine = jnp.cos(angles).reshape(samples, NB, 1, BIN)
-    sine_neg = (-jnp.sin(angles)).reshape(samples, NB, 1, BIN)
-    return (
-        jnp.concatenate([cosine, sine_neg], axis=2)
-        .reshape(samples, NB * 2 * BIN)
-        .astype(jnp.bfloat16)
-    )
-
-
-def per_device(records, quality, block_ids):
+def per_device_general(records, quality, block_ids):
     devices = lax.axis_size("rcv")
     groups = devices // NB
     windows, channels, samples = records.shape
@@ -64,7 +300,6 @@
         collected = jnp.concatenate([low_half, high_half], axis=0)
     slices = []
     for source_slot in range(NSB):
-        first_group = block_ids[source_slot] % per_block * blk_rows
         slices.append(collected[:, source_slot])
     src_band = jnp.stack(slices).reshape(NSB, blk_rows, windows, sub_rows, 2, BIN)
     source_count = NSB * SBLK
@@ -77,6 +312,25 @@
     return (joined * (1.0 / windows)).astype(jnp.bfloat16)[None]
 
 
+def per_device(records, quality, block_ids):
+    devices = lax.axis_size("rcv")
+    windows, channels, samples = records.shape
+    groups = devices // NB
+    sub_rows = channels // groups
+    pack = LANES // sub_rows
+    fits = (
+        groups == 2
+        and channels == SBLK
+        and windows == pack
+        and sub_rows * pack == LANES
+        and NSB * groups == pack
+        and devices % (2 * pack) == 0
+        and FLO % 2 == 0
+        and samples % 2 == 0
+    )
+    return (per_device_kernels if fits else per_device_general)(records, quality, block_ids)
+
+
 def solution(mesh):
     placed = (P("grp", "rcv", None), P("grp", "rcv"), P("grp"))
     return jax.shard_map(

time: 40.4 us -> 27.2 us (0.67)
  Pallas kernels: 0 us -> 23.2 us
  other arithmetic: 11 us -> 0 us
  starting transfers between devices: 7.46 us -> 0 us
  matrix products: 7.45 us -> 0 us
  waiting for transfers between devices: 5.62 us -> 0 us
  between operations: 4 us -> 0.01 us
  local copies, waits for them, and re-layouts: 4.52 us -> 3.78 us
    pallas_call x0 -> x2, Pallas kernels: none -> 23.2 us  [the longest x1 16.8 us: per_device_kernels(): pl.pallas_call(exchange_kernel, out_shape=(jax.ShapeDtypeStruct((2, plane...]
    another operation x1 -> x0, other arithmetic: 8.96 us -> none
    dot_general x2 -> x0, matrix products: 7.45 us -> none  [the longest x1 5.99 us: per_device(): jnp.einsum('inwp,iwpk->ink', left_side, right_side, preferred_element_typ...]
    all_to_all x1 -> x0, starting transfers between devices: 7.39 us -> none  [per_device(): lax.all_to_all(send_buf, 'rcv', split_axis=0, concat_axis=0, tiled=True)]
    all_to_all x1 -> x0, waiting for transfers between devices: 5.61 us -> none  [per_device(): lax.all_to_all(send_buf, 'rcv', split_axis=0, concat_axis=0, tiled=True)]
    unnamed x4 -> x8, local copies, waits for them, and re-layouts: 0.01 us -> 3.78 us
    reshape x5 -> x0, local copies, waits for them, and re-layouts: 2.92 us -> none  [the longest x2 1.13 us: per_device(): send_buf = whitened.reshape(devices, windows, sub_rows * 2 * BIN)]
    convert_element_type x2 -> x0, other arithmetic: 1.11 us -> none  [the longest x1 0.77 us: per_device(): quality.reshape(windows, groups, sub_rows).transpose(1, 0, 2)]
  transfers between devices with their start and end apart: 2 -> 0, of which waited for: 1 -> 0; matrix products, arithmetic and copies ran while one was open for 6% -> 0% of each run, Pallas kernels for 0% -> 0%
where the time goes in v1:
time: 27.2 us; the launch traced here: 26.9 us
  Pallas kernels  23.2 us (85%)
  local copies, waits for them, and re-layouts  3.78 us (14%)
    pallas_call x1, Pallas kernels, per_device_kernels(): pl.pallas_call(exchange_kernel, out_shape=(jax.ShapeDtypeStruct((2, plane...  16.8 us
    pallas_call x1, Pallas kernels, per_device_kernels(): pl.pallas_call(product_kernel, grid=(BIN // step_bins,), out_shape=jax.Sh...  6.34 us
    unnamed x8, local copies, waits for them, and re-layouts  3.78 us

profile of v1, /device:TPU:0, one launch (start us, length us, event | category | flops | bytes accessed | tf_op | source)
XLA Modules:
  0.0 26.9 jit_solution(2433672397357307363)
XLA Ops:
  0.0 0.0 copy-start
  0.0 1.2 %copy-done = bf16[4,64,2048]{2,1,0:T(8,128)(2,1)S(1)} copy-done((bf16[4,64,2048]{2,1,0:T(8,128)(2,1)S(1)}, bf16[4,64,2048]{2,1,0:T(8,128)(2,1)}, u32[]{:S(2)}) %copy-start) | copy-done | bytes 1048600
  1.2 0.0 copy-start.1
  1.2 1.2 %copy-done.1 = bf16[512,1024]{1,0:T(8,128)(2,1)S(1)} copy-done((bf16[512,1024]{1,0:T(8,128)(2,1)S(1)}, bf16[512,1024]{1,0:T(8,128)(2,1)}, u32[]{:S(2)}) %copy-start.1) | copy-done | bytes 1048600
  2.5 0.0 copy-start.2
  2.5 0.7 %copy-done.2 = s32[4,64]{1,0:T(4,128)S(1)} copy-done((s32[4,64]{1,0:T(4,128)S(1)}, s32[4,64]{1,0:T(4,128)}, u32[]{:S(2)}) %copy-start.2) | copy-done | bytes 1048
  3.1 0.0 copy-start.3
  3.1 0.7 %copy-done.3 = s32[2]{0:T(128)S(1)} copy-done((s32[2]{0:T(128)S(1)}, s32[2]{0:T(128)}, u32[]{:S(2)}) %copy-start.3) | copy-done | bytes 32
  3.8 16.8 %spectra_exchange.1 = (bf16[2,4,256,128]{3,2,1,0:T(8,128)(2,1)S(1)}, bf16[2,2,64,128]{3,2,1,0:T(8,128)(2,1)S(1)}) custom-call(s32[2]{0:T(128)S(1)} %copy-done.3, s32[4,64]{1,0:T(4,128)S(1)} %copy-done.2, bf16[512,1024]{1,0:T(8,128)(2,1)S(1)} %copy-done.1, bf16[4,64,2048]{2,1,0:T(8,128)(2,1)S(1)} %copy-done), custom_call_target="tpu_custom_call" | custom-call | tf_op jit(solution)/shard_map/spectra_exchange/pallas_call | solution.py:209
  20.6 6.3 %cross_spectra.1 = bf16[32,128,1024]{2,1,0:T(8,128)(2,1)} custom-call(bf16[2,2,64,128]{3,2,1,0:T(8,128)(2,1)S(1)} %get-tuple-element.7.src_ref, bf16[2,4,256,128]{3,2,1,0:T(8,128)(2,1)S(1)} %get-tuple-element.8.rhs_ref), custom_call_target="tpu_custom_call" | custom-call | tf_op jit(solution)/shard_map/cross_spectra/pallas_call | solution.py:243
Async XLA Ops:
  0.0 1.2 %copy-start = (bf16[4,64,2048]{2,1,0:T(8,128)(2,1)S(1)}, bf16[4,64,2048]{2,1,0:T(8,128)(2,1)}, u32[]{:S(2)}) copy-start(bf16[4,64,2048]{2,1,0:T(8,128)(2,1)} %records_ref.1) | copy-start | bytes 3145732
  1.2 1.2 %copy-start.1 = (bf16[512,1024]{1,0:T(8,128)(2,1)S(1)}, bf16[512,1024]{1,0:T(8,128)(2,1)}, u32[]{:S(2)}) copy-start(bf16[512,1024]{1,0:T(8,128)(2,1)} %constant.2.clone.basis_ref) | copy-start | bytes 3145732
  2.5 0.7 %copy-start.2 = (s32[4,64]{1,0:T(4,128)S(1)}, s32[4,64]{1,0:T(4,128)}, u32[]{:S(2)}) copy-start(s32[4,64]{1,0:T(4,128)} %quality_ref.1) | copy-start | bytes 3076
  3.1 0.7 %copy-start.3 = (s32[2]{0:T(128)S(1)}, s32[2]{0:T(128)}, u32[]{:S(2)}) copy-start(s32[2]{0:T(128)} %ids_ref.1) | copy-start | bytes 28

commit v2 on v1

--- a/solution.py
+++ b/solution.py
@@ -51,9 +51,9 @@
 
 
 def exchange_kernel(
-    ids_ref, quality_ref, basis_ref, records_ref, rhs_ref, src_ref,
-    basis_v, rec_v, send_v, recv_v, rhs_v, own_v,
-    load_sem, send_sem, recv_sem, plane_sem, src_sem,
+    small_ref, basis_ref, records_ref, rhs_ref, src_ref,
+    basis_v, rec_v, send_v, recv_v, own_v,
+    load_sem, basis_sem, send_sem, recv_sem, src_sem,
 ):
     devices = recv_v.shape[0]
     windows, channels, samples = records_ref.shape
@@ -65,7 +65,14 @@
     rows = 2 * BIN
     me = lax.axis_index("rcv")
 
-    loads = [pltpu.make_async_copy(basis_ref, basis_v, load_sem.at[0])]
+    barrier = pltpu.get_barrier_semaphore()
+    for off in range(1, devices):
+        pl.semaphore_signal(
+            barrier, inc=1, device_id={"rcv": flipped(me, off)},
+            device_id_type=pl.DeviceIdType.MESH,
+        )
+
+    loads = []
     for q in range(groups):
         for w in range(windows):
             place = q * windows + w
@@ -73,59 +80,62 @@
                 pltpu.make_async_copy(
                     records_ref.at[w, pl.ds(q * sub_rows, sub_rows)],
                     rec_v.at[pl.ds(place * sub_rows, sub_rows)],
-                    load_sem.at[1 + place],
+                    load_sem.at[place],
                 )
             )
+    near_side = me // (devices // 2)
+    sides = (1 - near_side, near_side)
+    side_rows = NB * rows // 2
+    basis_loads = []
+    for turn, side in enumerate(sides):
+        piece = pl.ds(pl.multiple_of(side * side_rows, side_rows), side_rows)
+        basis_loads.append(
+            pltpu.make_async_copy(basis_ref.at[piece], basis_v.at[turn], basis_sem.at[turn])
+        )
+    for load in loads + basis_loads:
+        load.start()
     for load in loads:
-        load.start()
-
-    barrier = pltpu.get_barrier_semaphore()
-    for off in range(1, devices):
-        pl.semaphore_signal(
-            barrier, inc=1, device_id={"rcv": flipped(me, off)},
-            device_id_type=pl.DeviceIdType.MESH,
-        )
+        load.wait()
 
     keep = jnp.concatenate(
         [
-            quality_ref[w : w + 1, q * sub_rows : (q + 1) * sub_rows]
+            small_ref[w : w + 1, q * sub_rows : (q + 1) * sub_rows]
             for q in range(groups)
             for w in range(windows)
         ],
         axis=1,
     ).astype(jnp.float32)
-    for load in loads:
-        load.wait()
-
     contract = (((1,), (1,)), ((), ()))
-    low = lax.dot_general(
-        basis_v[...], rec_v[:, :half], contract, preferred_element_type=jnp.float32
-    )
-    high = lax.dot_general(
-        basis_v[...], rec_v[:, half:], contract, preferred_element_type=jnp.float32
-    )
-    odd = lax.broadcasted_iota(jnp.int32, (rows, low.shape[1]), 0) % 2 == 1
-    for b in range(NB):
-        band = slice(b * rows, (b + 1) * rows)
-        spectrum = low[band] + jnp.where(odd, -high[band], high[band])
-        power = jnp.sum(spectrum * spectrum, axis=0, keepdims=True) / BIN
-        white = (spectrum * (keep * lax.rsqrt(power + 1e-05))).astype(jnp.bfloat16)
-        for q in range(groups):
-            send_v[b * groups + q] = white[:, q * LANES : (q + 1) * LANES]
-
-    pl.semaphore_wait(barrier, devices - 1)
+    odd = lax.broadcasted_iota(jnp.int32, (rows, keep.shape[1]), 0) % 2 == 1
     copies = {}
-    for off in range(devices - 1, 0, -1):
-        peer = flipped(me, off)
-        copies[off] = pltpu.make_async_remote_copy(
-            src_ref=send_v.at[peer], dst_ref=recv_v.at[me],
-            send_sem=send_sem.at[off], recv_sem=recv_sem.at[off],
-            device_id={"rcv": peer}, device_id_type=pl.DeviceIdType.MESH,
-        )
-        copies[off].start()
+    for turn, side in enumerate(sides):
+        basis_loads[turn].wait()
+        low = lax.dot_general(
+            basis_v[turn], rec_v[:, :half], contract, preferred_element_type=jnp.float32
+        )
+        high = lax.dot_general(
+            basis_v[turn], rec_v[:, half:], contract, preferred_element_type=jnp.float32
+        )
+        for b in range(NB // 2):
+            band = slice(b * rows, (b + 1) * rows)
+            spectrum = low[band] + jnp.where(odd, -high[band], high[band])
+            power = jnp.sum(spectrum * spectrum, axis=0, keepdims=True) / BIN
+            white = (spectrum * (keep * lax.rsqrt(power + 1e-05))).astype(jnp.bfloat16)
+            for q in range(groups):
+                send_v[side * (devices // 2) + b * groups + q] = white[:, q * LANES : (q + 1) * LANES]
+        if turn == 0:
+            pl.semaphore_wait(barrier, devices - 1)
+        offs = range(devices // 2, devices) if turn == 0 else range(1, devices // 2)
+        for off in reversed(offs):
+            peer = flipped(me, off)
+            copies[off] = pltpu.make_async_remote_copy(
+                src_ref=send_v.at[peer], dst_ref=recv_v.at[me],
+                send_sem=send_sem.at[off], recv_sem=recv_sem.at[off],
+                device_id={"rcv": peer}, device_id_type=pl.DeviceIdType.MESH,
+            )
+            copies[off].start()
     recv_v[me] = send_v[me]
 
-    outs = []
     for dz in range(planes):
         plane = flipped(me // pack, dz)
         for e in range(pack):
@@ -134,66 +144,73 @@
                 copies[off].wait_recv()
         if dz == planes - 1:
             for s in range(NSB):
-                own_v[s] = recv_v[ids_ref[s]]
+                own_v[s] = recv_v[small_ref[0, channels + s]]
             swap = pltpu.make_async_remote_copy(
                 src_ref=own_v, dst_ref=src_ref.at[me % groups],
                 send_sem=src_sem.at[0], recv_sem=src_sem.at[1],
                 device_id={"rcv": flipped(me, 1)}, device_id_type=pl.DeviceIdType.MESH,
             )
             swap.start()
-            keep_own = pltpu.make_async_copy(own_v, src_ref.at[me % groups], src_sem.at[2])
-            keep_own.start()
+            src_ref[me % groups] = own_v[...]
         by_window = lanes_to_rows([recv_v[plane * pack + e] for e in range(pack)], sub_rows)
         for w, block in enumerate(by_window):
             real, imag = block[:BIN], block[BIN:]
-            rhs_v[0, plane, w * rows : w * rows + BIN] = real.astype(jnp.bfloat16)
-            rhs_v[0, plane, w * rows + BIN : (w + 1) * rows] = imag.astype(jnp.bfloat16)
-            rhs_v[1, plane, w * rows : w * rows + BIN] = imag.astype(jnp.bfloat16)
-            rhs_v[1, plane, w * rows + BIN : (w + 1) * rows] = (-real).astype(jnp.bfloat16)
-        for part in range(2):
-            out = pltpu.make_async_copy(
-                rhs_v.at[part, plane], rhs_ref.at[part, plane], plane_sem.at[part, dz]
-            )
-            out.start()
-            outs.append(out)
+            rhs_ref[0, plane, w * rows : w * rows + BIN] = real.astype(jnp.bfloat16)
+            rhs_ref[0, plane, w * rows + BIN : (w + 1) * rows] = imag.astype(jnp.bfloat16)
+            rhs_ref[1, plane, w * rows : w * rows + BIN] = imag.astype(jnp.bfloat16)
+            rhs_ref[1, plane, w * rows + BIN : (w + 1) * rows] = (-real).astype(jnp.bfloat16)
     for off in range(devices - 1, 0, -1):
         copies[off].wait_send()
-    for out in outs:
-        out.wait()
-    keep_own.wait()
     swap.wait()
 
 
-def product_kernel(src_ref, rhs_ref, out_ref, left_v):
-    step = pl.program_id(0)
-    bins = out_ref.shape[0]
+STEP_BINS = 4
+
+
+def product_kernel(src_ref, rhs_ref, out_ref, left_v, out_v, out_sem):
     rows = 2 * BIN
+    planes = rhs_ref.shape[1]
     windows = rhs_ref.shape[2] // rows
     groups, blocks = src_ref.shape[:2]
     sub_rows = SBLK // groups
-
-    @pl.when(step == 0)
-    def _():
-        pieces = [src_ref[q, s] for s in range(blocks) for q in range(groups)]
-        by_window = lanes_to_rows(pieces, sub_rows)
-        left_v[...] = jnp.concatenate(by_window, axis=0).T * (1.0 / windows)
-
-    left = left_v[...]
-    bin_of = lax.broadcasted_iota(jnp.int32, left.shape, 1) % BIN
-    masked = jnp.concatenate(
-        [jnp.where(bin_of == step * bins + i, left, 0.0).astype(jnp.bfloat16) for i in range(bins)],
-        axis=0,
-    )
-    planes = rhs_ref.shape[1]
     wide = 2
-    for part in range(2):
-        for z in range(0, planes, wide):
-            right = jnp.concatenate([rhs_ref[part, z + u] for u in range(wide)], axis=1)
-            both = jnp.dot(masked, right, preferred_element_type=jnp.float32)
-            first = (part * planes + z) * LANES
-            out_ref[:, :, first : first + wide * LANES] = both.astype(jnp.bfloat16).reshape(
-                bins, left.shape[0], wide * LANES
-            )
+
+    pieces = [src_ref[q, s] for s in range(blocks) for q in range(groups)]
+    by_window = lanes_to_rows(pieces, sub_rows)
+    left_v[...] = jnp.concatenate(by_window, axis=0).T * (1.0 / windows)
+
+    def write(place):
+        return pltpu.make_async_copy(out_v.at[place], out_ref.at[place], out_sem.at[place])
+
+    def step_body(step, carry):
+        left = left_v[...]
+        bin_of = lax.broadcasted_iota(jnp.int32, left.shape, 1) % BIN
+        masked = jnp.concatenate(
+            [
+                jnp.where(bin_of == step * STEP_BINS + i, left, 0.0).astype(jnp.bfloat16)
+                for i in range(STEP_BINS)
+            ],
+            axis=0,
+        )
+        for part in range(2):
+            for z in range(0, planes, wide):
+                right = jnp.concatenate([rhs_ref[part, z + u] for u in range(wide)], axis=1)
+                both = jnp.dot(masked, right, preferred_element_type=jnp.float32)
+                first = (part * planes + z) * LANES
+                out_v[pl.ds(step * STEP_BINS, STEP_BINS), :, first : first + wide * LANES] = (
+                    both.astype(jnp.bfloat16).reshape(STEP_BINS, left.shape[0], wide * LANES)
+                )
+        for i in range(STEP_BINS):
+            write(step * STEP_BINS + i).start()
+        return carry
+
+    lax.fori_loop(0, BIN // STEP_BINS, step_body, 0)
+
+    def wait_body(place, carry):
+        write(place).wait()
+        return carry
+
+    lax.fori_loop(0, BIN, wait_body, 0)
 
 
 def per_device_kernels(records, quality, block_ids):
@@ -206,6 +223,8 @@
     rows = 2 * BIN
     depth = windows * rows
     basis = jnp.asarray(basis_rows(samples, samples // 2))
+    padded_ids = jnp.pad(block_ids.reshape(1, -1), ((0, windows - 1), (0, LANES - channels - NSB)))
+    small = jnp.concatenate([quality, padded_ids], axis=1)
     rhs, src = pl.pallas_call(
         exchange_kernel,
         out_shape=(
@@ -213,44 +232,42 @@
             jax.ShapeDtypeStruct((groups, NSB, rows, LANES), jnp.bfloat16),
         ),
         in_specs=[
-            pl.BlockSpec(memory_space=pltpu.SMEM),
             pl.BlockSpec(memory_space=pltpu.VMEM),
-            pl.BlockSpec(memory_space=pl.ANY),
-            pl.BlockSpec(memory_space=pl.ANY),
+            pl.BlockSpec(memory_space=pltpu.HBM),
+            pl.BlockSpec(memory_space=pltpu.HBM),
         ],
-        out_specs=(pl.BlockSpec(memory_space=pl.ANY), pl.BlockSpec(memory_space=pl.ANY)),
+        out_specs=(pl.BlockSpec(memory_space=pltpu.VMEM), pl.BlockSpec(memory_space=pltpu.VMEM)),
         scratch_shapes=[
-            pltpu.VMEM(basis.shape, jnp.bfloat16),
+            pltpu.VMEM((2, basis.shape[0] // 2, basis.shape[1]), jnp.bfloat16),
             pltpu.VMEM((windows * channels, samples), jnp.bfloat16),
             pltpu.VMEM((devices, rows, LANES), jnp.bfloat16),
             pltpu.VMEM((devices, rows, LANES), jnp.bfloat16),
-            pltpu.VMEM((2, planes, depth, LANES), jnp.bfloat16),
             pltpu.VMEM((NSB, rows, LANES), jnp.bfloat16),
-            pltpu.SemaphoreType.DMA((1 + groups * windows,)),
+            pltpu.SemaphoreType.DMA((groups * windows,)),
+            pltpu.SemaphoreType.DMA((2,)),
             pltpu.SemaphoreType.DMA((devices,)),
             pltpu.SemaphoreType.DMA((devices,)),
-            pltpu.SemaphoreType.DMA((2, planes)),
-            pltpu.SemaphoreType.DMA((3,)),
+            pltpu.SemaphoreType.DMA((2,)),
         ],
         compiler_params=pltpu.CompilerParams(
-            collective_id=0, has_side_effects=True, vmem_limit_bytes=32 * 2**20
+            collective_id=0, has_side_effects=True, vmem_limit_bytes=53 * 2**20
         ),
         name="spectra_exchange",
-    )(block_ids, quality, basis, records)
+    )(small, basis, records)
 
     count = NSB * SBLK
-    step_bins = 4
+    out_shape = (BIN, count, 2 * planes * LANES)
     joined = pl.pallas_call(
         product_kernel,
-        grid=(BIN // step_bins,),
-        out_shape=jax.ShapeDtypeStruct((BIN, count, 2 * planes * LANES), jnp.bfloat16),
-        in_specs=[
-            pl.BlockSpec(src.shape, lambda i: (0, 0, 0, 0)),
-            pl.BlockSpec(rhs.shape, lambda i: (0, 0, 0, 0)),
+        out_shape=jax.ShapeDtypeStruct(out_shape, jnp.bfloat16),
+        in_specs=[pl.BlockSpec(memory_space=pltpu.VMEM)] * 2,
+        out_specs=pl.BlockSpec(memory_space=pltpu.HBM),
+        scratch_shapes=[
+            pltpu.VMEM((count, depth), jnp.float32),
+            pltpu.VMEM(out_shape, jnp.bfloat16),
+            pltpu.SemaphoreType.DMA((BIN,)),
         ],
-        out_specs=pl.BlockSpec((step_bins, count, 2 * planes * LANES), lambda i: (i, 0, 0)),
-        scratch_shapes=[pltpu.VMEM((count, depth), jnp.float32)],
-        compiler_params=pltpu.CompilerParams(vmem_limit_bytes=32 * 2**20),
+        compiler_params=pltpu.CompilerParams(vmem_limit_bytes=40 * 2**20),
         name="cross_spectra",
     )(src, rhs)
     return joined[None]

time: 27.2 us -> 20.6 us (0.76)
  local copies, waits for them, and re-layouts: 3.78 us -> 0 us
  Pallas kernels: 23.2 us -> 19.7 us
  other arithmetic: 0 us -> 0.77 us
    unnamed x8 -> x0, local copies, waits for them, and re-layouts: 3.78 us -> none
    pallas_call x1, Pallas kernels: 16.8 us -> 14.7 us  [per_device_kernels(): pl.pallas_call(exchange_kernel, out_shape=(jax.ShapeDtypeStruct((2, plane...]
    pallas_call x1, Pallas kernels: 6.34 us -> 4.99 us  [per_device_kernels(): pl.pallas_call(product_kernel, out_shape=jax.ShapeDtypeStruct(out_shape,...]
    concatenate x0 -> x1, other arithmetic: none -> 0.77 us  [per_device_kernels(): small = jnp.concatenate([quality, padded_ids], axis=1)]
where the time goes in v2:
time: 20.6 us; the launch traced here: 20.5 us
  Pallas kernels  19.7 us (96%)
  other arithmetic  0.77 us (4%)
    pallas_call x1, Pallas kernels, per_device_kernels(): pl.pallas_call(exchange_kernel, out_shape=(jax.ShapeDtypeStruct((2, plane...  14.7 us
    pallas_call x1, Pallas kernels, per_device_kernels(): pl.pallas_call(product_kernel, out_shape=jax.ShapeDtypeStruct(out_shape,...  4.99 us
    concatenate x1, other arithmetic, per_device_kernels(): small = jnp.concatenate([quality, padded_ids], axis=1)  0.77 us

profile of v2, /device:TPU:0, one launch (start us, length us, event | category | flops | bytes accessed | tf_op | source)
XLA Modules:
  0.0 20.5 jit_solution(14585451892650040799)
XLA Ops:
  0.0 0.8 %pad_add_fusion.small_ref = s32[4,128]{1,0:T(4,128)S(1)} fusion(s32[1,2]{1,0:T(1,128)} %bitcast.2, s32[4,64]{1,0:T(4,128)} %param.5), kind=kLoop, calls=%fused_computation | loop fusion | flops 512 | bytes 3080 | tf_op jit(solution)/shard_map/concatenate | solution.py:227
  0.8 14.7 %spectra_exchange.1 = (bf16[2,4,256,128]{3,2,1,0:T(8,128)(2,1)S(1)}, bf16[2,2,64,128]{3,2,1,0:T(8,128)(2,1)S(1)}) custom-call(s32[4,128]{1,0:T(4,128)S(1)} %pad_add_fusion.small_ref, bf16[512,1024]{1,0:T(8,128)(2,1)} %constant.4.clone.basis_ref, bf16[4,64,2048]{2,1,0:T(8,128)(2,1)} %records_ref.1), custom_call_target="tpu_custom_call" | custom-call | tf_op jit(solution)/shard_map/spectra_exchange/pallas_call | solution.py:228
  15.5 5.0 %cross_spectra.1 = bf16[32,128,1024]{2,1,0:T(8,128)(2,1)} custom-call(bf16[2,2,64,128]{3,2,1,0:T(8,128)(2,1)S(1)} %get-tuple-element.7.src_ref, bf16[2,4,256,128]{3,2,1,0:T(8,128)(2,1)S(1)} %get-tuple-element.8.rhs_ref), custom_call_target="tpu_custom_call" | custom-call | tf_op jit(solution)/shard_map/cross_spectra/pallas_call | solution.py:260

commit v3 on v2

--- a/solution.py
+++ b/solution.py
@@ -17,13 +17,13 @@
 LANES = 128
 
 
-def basis_rows(samples, count):
+def basis_table(samples, count):
     times = np.arange(count, dtype=np.int64)
     bins = FLO + np.arange(NB * BIN, dtype=np.int64)
-    phases = (bins[:, None] * times[None, :]) % samples
+    phases = (times[:, None] * bins[None, :]) % samples
     angles = phases.astype(np.float64) * (2.0 * np.pi / samples)
-    table = np.stack([np.cos(angles), -np.sin(angles)]).reshape(2, NB, BIN, count)
-    table = table.transpose(1, 0, 2, 3).reshape(NB * 2 * BIN, count)
+    table = np.stack([np.cos(angles), -np.sin(angles)]).reshape(2, count, NB, BIN)
+    table = table.transpose(1, 2, 0, 3).reshape(count, NB * 2 * BIN)
     return table.astype(np.float32).astype(ml_dtypes.bfloat16)
 
 
@@ -76,24 +76,22 @@
     for q in range(groups):
         for w in range(windows):
             place = q * windows + w
-            loads.append(
-                pltpu.make_async_copy(
-                    records_ref.at[w, pl.ds(q * sub_rows, sub_rows)],
-                    rec_v.at[pl.ds(place * sub_rows, sub_rows)],
-                    load_sem.at[place],
+            for h in range(2):
+                loads.append(
+                    pltpu.make_async_copy(
+                        records_ref.at[w, pl.ds(q * sub_rows, sub_rows), pl.ds(h * half, half)],
+                        rec_v.at[h, pl.ds(place * sub_rows, sub_rows)],
+                        load_sem.at[2 * place + h],
+                    )
                 )
-            )
     near_side = me // (devices // 2)
     sides = (1 - near_side, near_side)
-    side_rows = NB * rows // 2
-    basis_loads = []
-    for turn, side in enumerate(sides):
-        piece = pl.ds(pl.multiple_of(side * side_rows, side_rows), side_rows)
-        basis_loads.append(
-            pltpu.make_async_copy(basis_ref.at[piece], basis_v.at[turn], basis_sem.at[turn])
-        )
-    for load in loads + basis_loads:
-        load.start()
+    basis_loads = [
+        pltpu.make_async_copy(basis_ref.at[side], basis_v.at[turn], basis_sem.at[turn])
+        for turn, side in enumerate(sides)
+    ]
+    for turn, load in enumerate([basis_loads[0]] + loads + [basis_loads[1]]):
+        load.start(priority=turn % 2)
     for load in loads:
         load.wait()
 
@@ -105,44 +103,54 @@
         ],
         axis=1,
     ).astype(jnp.float32)
-    contract = (((1,), (1,)), ((), ()))
-    odd = lax.broadcasted_iota(jnp.int32, (rows, keep.shape[1]), 0) % 2 == 1
-    copies = {}
+    count = windows * channels
+
+    def remote(peer):
+        return pltpu.make_async_remote_copy(
+            src_ref=send_v.at[peer], dst_ref=recv_v.at[me],
+            send_sem=send_sem.at[peer], recv_sem=recv_sem.at[me],
+            device_id={"rcv": peer}, device_id_type=pl.DeviceIdType.MESH,
+        )
+
+    def arrival(peer):
+        return pltpu.make_async_remote_copy(
+            src_ref=send_v.at[peer], dst_ref=recv_v.at[peer],
+            send_sem=send_sem.at[peer], recv_sem=recv_sem.at[peer],
+            device_id={"rcv": peer}, device_id_type=pl.DeviceIdType.MESH,
+        )
+
+    my_plane, my_place = me // pack, me % pack
+    far_planes = [
+        near_side * u + (1 - near_side) * (planes - 1 - u) for u in range(planes // 2)
+    ]
+    near_planes = [flipped(my_plane, u) for u in range(planes // 2 - 1, -1, -1)]
     for turn, side in enumerate(sides):
         basis_loads[turn].wait()
-        low = lax.dot_general(
-            basis_v[turn], rec_v[:, :half], contract, preferred_element_type=jnp.float32
-        )
-        high = lax.dot_general(
-            basis_v[turn], rec_v[:, half:], contract, preferred_element_type=jnp.float32
-        )
+        halves = jnp.dot(
+            rec_v[...].reshape(2 * count, half), basis_v[turn], preferred_element_type=jnp.float32
+        )
+        odd = lax.broadcasted_iota(jnp.int32, (count, halves.shape[1]), 1) % 2 == 1
+        late = halves[count:]
+        spectra = (halves[:count] + jnp.where(odd, -late, late)).T
         for b in range(NB // 2):
-            band = slice(b * rows, (b + 1) * rows)
-            spectrum = low[band] + jnp.where(odd, -high[band], high[band])
+            spectrum = spectra[b * rows : (b + 1) * rows]
             power = jnp.sum(spectrum * spectrum, axis=0, keepdims=True) / BIN
             white = (spectrum * (keep * lax.rsqrt(power + 1e-05))).astype(jnp.bfloat16)
             for q in range(groups):
                 send_v[side * (devices // 2) + b * groups + q] = white[:, q * LANES : (q + 1) * LANES]
         if turn == 0:
             pl.semaphore_wait(barrier, devices - 1)
-        offs = range(devices // 2, devices) if turn == 0 else range(1, devices // 2)
-        for off in reversed(offs):
-            peer = flipped(me, off)
-            copies[off] = pltpu.make_async_remote_copy(
-                src_ref=send_v.at[peer], dst_ref=recv_v.at[me],
-                send_sem=send_sem.at[off], recv_sem=recv_sem.at[off],
-                device_id={"rcv": peer}, device_id_type=pl.DeviceIdType.MESH,
-            )
-            copies[off].start()
+        for plane in far_planes if turn == 0 else near_planes:
+            own = turn == 1 and plane is near_planes[-1]
+            for e in range(pack - 1, 0 if own else -1, -1):
+                remote(plane * pack + flipped(my_place, e)).start()
     recv_v[me] = send_v[me]
 
-    for dz in range(planes):
-        plane = flipped(me // pack, dz)
-        for e in range(pack):
-            off = dz * pack + e
-            if off:
-                copies[off].wait_recv()
-        if dz == planes - 1:
+    ordered = near_planes[::-1] + far_planes
+    for turn, plane in enumerate(ordered):
+        for e in range(0 if turn else 1, pack):
+            arrival(plane * pack + flipped(my_place, e)).wait_recv()
+        if turn == planes - 1:
             for s in range(NSB):
                 own_v[s] = recv_v[small_ref[0, channels + s]]
             swap = pltpu.make_async_remote_copy(
@@ -159,8 +167,8 @@
             rhs_ref[0, plane, w * rows + BIN : (w + 1) * rows] = imag.astype(jnp.bfloat16)
             rhs_ref[1, plane, w * rows : w * rows + BIN] = imag.astype(jnp.bfloat16)
             rhs_ref[1, plane, w * rows + BIN : (w + 1) * rows] = (-real).astype(jnp.bfloat16)
-    for off in range(devices - 1, 0, -1):
-        copies[off].wait_send()
+    for off in range(1, devices):
+        remote(flipped(me, off)).wait_send()
     swap.wait()
 
 
@@ -201,7 +209,7 @@
                     both.astype(jnp.bfloat16).reshape(STEP_BINS, left.shape[0], wide * LANES)
                 )
         for i in range(STEP_BINS):
-            write(step * STEP_BINS + i).start()
+            write(step * STEP_BINS + i).start(priority=i % 2)
         return carry
 
     lax.fori_loop(0, BIN // STEP_BINS, step_body, 0)
@@ -222,7 +230,8 @@
     planes = devices // pack
     rows = 2 * BIN
     depth = windows * rows
-    basis = jnp.asarray(basis_rows(samples, samples // 2))
+    table = basis_table(samples, samples // 2).reshape(samples // 2, 2, NB * BIN)
+    basis = jnp.asarray(np.ascontiguousarray(table.transpose(1, 0, 2)))
     padded_ids = jnp.pad(block_ids.reshape(1, -1), ((0, windows - 1), (0, LANES - channels - NSB)))
     small = jnp.concatenate([quality, padded_ids], axis=1)
     rhs, src = pl.pallas_call(
@@ -238,12 +247,12 @@
         ],
         out_specs=(pl.BlockSpec(memory_space=pltpu.VMEM), pl.BlockSpec(memory_space=pltpu.VMEM)),
         scratch_shapes=[
-            pltpu.VMEM((2, basis.shape[0] // 2, basis.shape[1]), jnp.bfloat16),
-            pltpu.VMEM((windows * channels, samples), jnp.bfloat16),
+            pltpu.VMEM(basis.shape, jnp.bfloat16),
+            pltpu.VMEM((2, windows * channels, samples // 2), jnp.bfloat16),
             pltpu.VMEM((devices, rows, LANES), jnp.bfloat16),
             pltpu.VMEM((devices, rows, LANES), jnp.bfloat16),
             pltpu.VMEM((NSB, rows, LANES), jnp.bfloat16),
-            pltpu.SemaphoreType.DMA((groups * windows,)),
+            pltpu.SemaphoreType.DMA((2 * groups * windows,)),
             pltpu.SemaphoreType.DMA((2,)),
             pltpu.SemaphoreType.DMA((devices,)),
             pltpu.SemaphoreType.DMA((devices,)),
@@ -274,7 +283,7 @@
 
 
 def make_basis(samples):
-    return jnp.asarray(basis_rows(samples, samples).T)
+    return jnp.asarray(basis_table(samples, samples))
 
 
 def from_partner(value, axis, stride):

time: 20.6 us -> 19.6 us (0.951)
  Pallas kernels: 19.7 us -> 18.7 us
    pallas_call x1, Pallas kernels: 14.7 us -> 13.7 us  [per_device_kernels(): pl.pallas_call(exchange_kernel, out_shape=(jax.ShapeDtypeStruct((2, plane...]
where the time goes in v3:
time: 19.6 us; the launch traced here: 19.5 us
  Pallas kernels  18.7 us (95%)
  other arithmetic  0.77 us (4%)
    pallas_call x1, Pallas kernels, per_device_kernels(): pl.pallas_call(exchange_kernel, out_shape=(jax.ShapeDtypeStruct((2, plane...  13.7 us
    pallas_call x1, Pallas kernels, per_device_kernels(): pl.pallas_call(product_kernel, out_shape=jax.ShapeDtypeStruct(out_shape,...  4.99 us
    concatenate x1, other arithmetic, per_device_kernels(): small = jnp.concatenate([quality, padded_ids], axis=1)  0.77 us

profile of v3, /device:TPU:0, one launch (start us, length us, event | category | flops | bytes accessed | tf_op | source)
XLA Modules:
  0.0 19.5 jit_solution(5235183298230698962)
XLA Ops:
  0.0 0.8 %pad_add_fusion.small_ref = s32[4,128]{1,0:T(4,128)S(1)} fusion(s32[1,2]{1,0:T(1,128)} %bitcast.2, s32[4,64]{1,0:T(4,128)} %param.5), kind=kLoop, calls=%fused_computation | loop fusion | flops 512 | bytes 3080 | tf_op jit(solution)/shard_map/concatenate | solution.py:236
  0.8 13.7 %spectra_exchange.1 = (bf16[2,4,256,128]{3,2,1,0:T(8,128)(2,1)S(1)}, bf16[2,2,64,128]{3,2,1,0:T(8,128)(2,1)S(1)}) custom-call(s32[4,128]{1,0:T(4,128)S(1)} %pad_add_fusion.small_ref, bf16[2,1024,256]{2,1,0:T(8,128)(2,1)} %constant.4.clone.basis_ref, bf16[4,64,2048]{2,1,0:T(8,128)(2,1)} %records_ref.1), custom_call_target="tpu_custom_call" | custom-call | tf_op jit(solution)/shard_map/spectra_exchange/pallas_call | solution.py:237
  14.5 5.0 %cross_spectra.1 = bf16[32,128,1024]{2,1,0:T(8,128)(2,1)} custom-call(bf16[2,2,64,128]{3,2,1,0:T(8,128)(2,1)S(1)} %get-tuple-element.7.src_ref, bf16[2,4,256,128]{3,2,1,0:T(8,128)(2,1)S(1)} %get-tuple-element.8.rhs_ref), custom_call_target="tpu_custom_call" | custom-call | tf_op jit(solution)/shard_map/cross_spectra/pallas_call | solution.py:269

commit v4 on v3

--- a/solution.py
+++ b/solution.py
@@ -190,7 +190,7 @@
     def write(place):
         return pltpu.make_async_copy(out_v.at[place], out_ref.at[place], out_sem.at[place])
 
-    def step_body(step, carry):
+    for step in range(BIN // STEP_BINS):
         left = left_v[...]
         bin_of = lax.broadcasted_iota(jnp.int32, left.shape, 1) % BIN
         masked = jnp.concatenate(
@@ -210,9 +210,6 @@
                 )
         for i in range(STEP_BINS):
             write(step * STEP_BINS + i).start(priority=i % 2)
-        return carry
-
-    lax.fori_loop(0, BIN // STEP_BINS, step_body, 0)
 
     def wait_body(place, carry):
         write(place).wait()

time: 19.6 us -> 18.7 us (0.954)
  Pallas kernels: 18.7 us -> 17.8 us
    pallas_call x1, Pallas kernels: 4.99 us -> 4.11 us  [per_device_kernels(): pl.pallas_call(product_kernel, out_shape=jax.ShapeDtypeStruct(out_shape,...]
where the time goes in v4:
time: 18.7 us; the launch traced here: 18.6 us
  Pallas kernels  17.8 us (95%)
  other arithmetic  0.77 us (4%)
    pallas_call x1, Pallas kernels, per_device_kernels(): pl.pallas_call(exchange_kernel, out_shape=(jax.ShapeDtypeStruct((2, plane...  13.7 us
    pallas_call x1, Pallas kernels, per_device_kernels(): pl.pallas_call(product_kernel, out_shape=jax.ShapeDtypeStruct(out_shape,...  4.11 us
    concatenate x1, other arithmetic, per_device_kernels(): small = jnp.concatenate([quality, padded_ids], axis=1)  0.77 us

profile of v4, /device:TPU:0, one launch (start us, length us, event | category | flops | bytes accessed | tf_op | source)
XLA Modules:
  0.0 18.6 jit_solution(15429919775246091143)
XLA Ops:
  0.0 0.8 %pad_add_fusion.small_ref = s32[4,128]{1,0:T(4,128)S(1)} fusion(s32[1,2]{1,0:T(1,128)} %bitcast.2, s32[4,64]{1,0:T(4,128)} %param.5), kind=kLoop, calls=%fused_computation | loop fusion | flops 512 | bytes 3080 | tf_op jit(solution)/shard_map/concatenate | solution.py:233
  0.8 13.7 %spectra_exchange.1 = (bf16[2,4,256,128]{3,2,1,0:T(8,128)(2,1)S(1)}, bf16[2,2,64,128]{3,2,1,0:T(8,128)(2,1)S(1)}) custom-call(s32[4,128]{1,0:T(4,128)S(1)} %pad_add_fusion.small_ref, bf16[2,1024,256]{2,1,0:T(8,128)(2,1)} %constant.4.clone.basis_ref, bf16[4,64,2048]{2,1,0:T(8,128)(2,1)} %records_ref.1), custom_call_target="tpu_custom_call" | custom-call | tf_op jit(solution)/shard_map/spectra_exchange/pallas_call | solution.py:234
  14.5 4.1 %cross_spectra.1 = bf16[32,128,1024]{2,1,0:T(8,128)(2,1)} custom-call(bf16[2,2,64,128]{3,2,1,0:T(8,128)(2,1)S(1)} %get-tuple-element.7.src_ref, bf16[2,4,256,128]{3,2,1,0:T(8,128)(2,1)S(1)} %get-tuple-element.8.rhs_ref), custom_call_target="tpu_custom_call" | custom-call | tf_op jit(solution)/shard_map/cross_spectra/pallas_call | solution.py:266

commit v5 on v4

--- a/solution.py
+++ b/solution.py
@@ -15,6 +15,7 @@
 SBLK = 64
 NSB = 2
 LANES = 128
+TIME_BLOCKS = 2
 
 
 def basis_table(samples, count):
@@ -72,37 +73,40 @@
             device_id_type=pl.DeviceIdType.MESH,
         )
 
-    loads = []
-    for q in range(groups):
-        for w in range(windows):
-            place = q * windows + w
-            for h in range(2):
-                loads.append(
-                    pltpu.make_async_copy(
-                        records_ref.at[w, pl.ds(q * sub_rows, sub_rows), pl.ds(h * half, half)],
-                        rec_v.at[h, pl.ds(place * sub_rows, sub_rows)],
-                        load_sem.at[2 * place + h],
-                    )
-                )
     near_side = me // (devices // 2)
     sides = (1 - near_side, near_side)
-    basis_loads = [
-        pltpu.make_async_copy(basis_ref.at[side], basis_v.at[turn], basis_sem.at[turn])
-        for turn, side in enumerate(sides)
-    ]
-    for turn, load in enumerate([basis_loads[0]] + loads + [basis_loads[1]]):
-        load.start(priority=turn % 2)
-    for load in loads:
-        load.wait()
-
-    keep = jnp.concatenate(
-        [
-            small_ref[w : w + 1, q * sub_rows : (q + 1) * sub_rows]
-            for q in range(groups)
-            for w in range(windows)
-        ],
-        axis=1,
-    ).astype(jnp.float32)
+    part = half // TIME_BLOCKS
+
+    def basis_load(turn, block):
+        piece = pl.ds(block * part, part)
+        return pltpu.make_async_copy(
+            basis_ref.at[sides[turn], piece], basis_v.at[turn, piece], basis_sem.at[turn, block]
+        )
+
+    def record_loads(block):
+        result = []
+        for q in range(groups):
+            for w in range(windows):
+                place = q * windows + w
+                for h in range(2):
+                    result.append(
+                        pltpu.make_async_copy(
+                            records_ref.at[
+                                w, pl.ds(q * sub_rows, sub_rows), pl.ds(h * half + block * part, part)
+                            ],
+                            rec_v.at[block, h, pl.ds(place * sub_rows, sub_rows)],
+                            load_sem.at[block, 2 * place + h],
+                        )
+                    )
+        return result
+
+    for block in range(TIME_BLOCKS):
+        basis_load(0, block).start()
+        for turn, load in enumerate(record_loads(block)):
+            load.start(priority=turn % 2)
+    for block in range(TIME_BLOCKS):
+        basis_load(1, block).start()
+
     count = windows * channels
 
     def remote(peer):
@@ -125,10 +129,26 @@
     ]
     near_planes = [flipped(my_plane, u) for u in range(planes // 2 - 1, -1, -1)]
     for turn, side in enumerate(sides):
-        basis_loads[turn].wait()
-        halves = jnp.dot(
-            rec_v[...].reshape(2 * count, half), basis_v[turn], preferred_element_type=jnp.float32
-        )
+        halves = 0.0
+        for block in range(TIME_BLOCKS):
+            basis_load(turn, block).wait()
+            if turn == 0:
+                for load in record_loads(block):
+                    load.wait()
+            halves = halves + jnp.dot(
+                rec_v[block].reshape(2 * count, part),
+                basis_v[turn, block * part : (block + 1) * part],
+                preferred_element_type=jnp.float32,
+            )
+        if turn == 0:
+            keep = jnp.concatenate(
+                [
+                    small_ref[w : w + 1, q * sub_rows : (q + 1) * sub_rows]
+                    for q in range(groups)
+                    for w in range(windows)
+                ],
+                axis=1,
+            ).astype(jnp.float32)
         odd = lax.broadcasted_iota(jnp.int32, (count, halves.shape[1]), 1) % 2 == 1
         late = halves[count:]
         spectra = (halves[:count] + jnp.where(odd, -late, late)).T
@@ -172,7 +192,13 @@
     swap.wait()
 
 
-STEP_BINS = 4
+def bin_steps():
+    first, steps = 0, []
+    while first < BIN:
+        width = min(8, max(2, first), BIN - first)
+        steps.append((first, width))
+        first += width
+    return steps
 
 
 def product_kernel(src_ref, rhs_ref, out_ref, left_v, out_v, out_sem):
@@ -190,13 +216,13 @@
     def write(place):
         return pltpu.make_async_copy(out_v.at[place], out_ref.at[place], out_sem.at[place])
 
-    for step in range(BIN // STEP_BINS):
+    for begin, bins in bin_steps():
         left = left_v[...]
         bin_of = lax.broadcasted_iota(jnp.int32, left.shape, 1) % BIN
         masked = jnp.concatenate(
             [
-                jnp.where(bin_of == step * STEP_BINS + i, left, 0.0).astype(jnp.bfloat16)
-                for i in range(STEP_BINS)
+                jnp.where(bin_of == begin + i, left, 0.0).astype(jnp.bfloat16)
+                for i in range(bins)
             ],
             axis=0,
         )
@@ -205,11 +231,11 @@
                 right = jnp.concatenate([rhs_ref[part, z + u] for u in range(wide)], axis=1)
                 both = jnp.dot(masked, right, preferred_element_type=jnp.float32)
                 first = (part * planes + z) * LANES
-                out_v[pl.ds(step * STEP_BINS, STEP_BINS), :, first : first + wide * LANES] = (
-                    both.astype(jnp.bfloat16).reshape(STEP_BINS, left.shape[0], wide * LANES)
+                out_v[begin : begin + bins, :, first : first + wide * LANES] = (
+                    both.astype(jnp.bfloat16).reshape(bins, left.shape[0], wide * LANES)
                 )
-        for i in range(STEP_BINS):
-            write(step * STEP_BINS + i).start(priority=i % 2)
+        for i in range(bins):
+            write(begin + i).start(priority=i % 2)
 
     def wait_body(place, carry):
         write(place).wait()
@@ -245,12 +271,14 @@
         out_specs=(pl.BlockSpec(memory_space=pltpu.VMEM), pl.BlockSpec(memory_space=pltpu.VMEM)),
         scratch_shapes=[
             pltpu.VMEM(basis.shape, jnp.bfloat16),
-            pltpu.VMEM((2, windows * channels, samples // 2), jnp.bfloat16),
+            pltpu.VMEM(
+                (TIME_BLOCKS, 2, windows * channels, samples // 2 // TIME_BLOCKS), jnp.bfloat16
+            ),
             pltpu.VMEM((devices, rows, LANES), jnp.bfloat16),
             pltpu.VMEM((devices, rows, LANES), jnp.bfloat16),
             pltpu.VMEM((NSB, rows, LANES), jnp.bfloat16),
-            pltpu.SemaphoreType.DMA((2 * groups * windows,)),
-            pltpu.SemaphoreType.DMA((2,)),
+            pltpu.SemaphoreType.DMA((TIME_BLOCKS, 2 * groups * windows)),
+            pltpu.SemaphoreType.DMA((2, TIME_BLOCKS)),
             pltpu.SemaphoreType.DMA((devices,)),
             pltpu.SemaphoreType.DMA((devices,)),
             pltpu.SemaphoreType.DMA((2,)),

time: 18.7 us -> 19 us (1.016)
  Pallas kernels: 17.8 us -> 18.1 us
where the time goes in v5:
time: 19 us; the launch traced here: 18.9 us
  Pallas kernels  18.1 us (95%)
  other arithmetic  0.77 us (4%)
    pallas_call x1, Pallas kernels, per_device_kernels(): pl.pallas_call(exchange_kernel, out_shape=(jax.ShapeDtypeStruct((2, plane...  13.9 us
    pallas_call x1, Pallas kernels, per_device_kernels(): pl.pallas_call(product_kernel, out_shape=jax.ShapeDtypeStruct(out_shape,...  4.24 us
    concatenate x1, other arithmetic, per_device_kernels(): small = jnp.concatenate([quality, padded_ids], axis=1)  0.77 us

profile of v5, /device:TPU:0, one launch (start us, length us, event | category | flops | bytes accessed | tf_op | source)
XLA Modules:
  0.0 18.9 jit_solution(13334583619292700938)
XLA Ops:
  0.0 0.8 %pad_add_fusion.small_ref = s32[4,128]{1,0:T(4,128)S(1)} fusion(s32[1,2]{1,0:T(1,128)} %bitcast.2, s32[4,64]{1,0:T(4,128)} %param.5), kind=kLoop, calls=%fused_computation | loop fusion | flops 512 | bytes 3080 | tf_op jit(solution)/shard_map/concatenate | solution.py:259
  0.8 13.9 %spectra_exchange.1 = (bf16[2,4,256,128]{3,2,1,0:T(8,128)(2,1)S(1)}, bf16[2,2,64,128]{3,2,1,0:T(8,128)(2,1)S(1)}) custom-call(s32[4,128]{1,0:T(4,128)S(1)} %pad_add_fusion.small_ref, bf16[2,1024,256]{2,1,0:T(8,128)(2,1)} %constant.4.clone.basis_ref, bf16[4,64,2048]{2,1,0:T(8,128)(2,1)} %records_ref.1), custom_call_target="tpu_custom_call" | custom-call | tf_op jit(solution)/shard_map/spectra_exchange/pallas_call | solution.py:260
  14.6 4.2 %cross_spectra.1 = bf16[32,128,1024]{2,1,0:T(8,128)(2,1)} custom-call(bf16[2,2,64,128]{3,2,1,0:T(8,128)(2,1)S(1)} %get-tuple-element.7.src_ref, bf16[2,4,256,128]{3,2,1,0:T(8,128)(2,1)S(1)} %get-tuple-element.8.rhs_ref), custom_call_target="tpu_custom_call" | custom-call | tf_op jit(solution)/shard_map/cross_spectra/pallas_call | solution.py:294

commit v6 on v4

--- a/solution.py
+++ b/solution.py
@@ -72,38 +72,29 @@
             device_id_type=pl.DeviceIdType.MESH,
         )
 
-    loads = []
-    for q in range(groups):
-        for w in range(windows):
-            place = q * windows + w
-            for h in range(2):
-                loads.append(
-                    pltpu.make_async_copy(
-                        records_ref.at[w, pl.ds(q * sub_rows, sub_rows), pl.ds(h * half, half)],
-                        rec_v.at[h, pl.ds(place * sub_rows, sub_rows)],
-                        load_sem.at[2 * place + h],
-                    )
-                )
     near_side = me // (devices // 2)
     sides = (1 - near_side, near_side)
     basis_loads = [
         pltpu.make_async_copy(basis_ref.at[side], basis_v.at[turn], basis_sem.at[turn])
         for turn, side in enumerate(sides)
     ]
-    for turn, load in enumerate([basis_loads[0]] + loads + [basis_loads[1]]):
-        load.start(priority=turn % 2)
-    for load in loads:
-        load.wait()
-
-    keep = jnp.concatenate(
-        [
-            small_ref[w : w + 1, q * sub_rows : (q + 1) * sub_rows]
-            for q in range(groups)
-            for w in range(windows)
-        ],
-        axis=1,
-    ).astype(jnp.float32)
-    count = windows * channels
+    loads = []
+    for q in range(groups):
+        loads.append([])
+        for w in range(windows):
+            for h in range(2):
+                loads[q].append(
+                    pltpu.make_async_copy(
+                        records_ref.at[w, pl.ds(q * sub_rows, sub_rows), pl.ds(h * half, half)],
+                        rec_v.at[q, h, pl.ds(w * sub_rows, sub_rows)],
+                        load_sem.at[q, 2 * w + h],
+                    )
+                )
+    basis_loads[0].start()
+    for group_loads in loads:
+        for turn, load in enumerate(group_loads):
+            load.start(priority=turn % 2)
+    basis_loads[1].start()
 
     def remote(peer):
         return pltpu.make_async_remote_copy(
@@ -124,26 +115,36 @@
         near_side * u + (1 - near_side) * (planes - 1 - u) for u in range(planes // 2)
     ]
     near_planes = [flipped(my_plane, u) for u in range(planes // 2 - 1, -1, -1)]
+    odd = lax.broadcasted_iota(jnp.int32, (LANES, NB * BIN), 1) % 2 == 1
     for turn, side in enumerate(sides):
         basis_loads[turn].wait()
-        halves = jnp.dot(
-            rec_v[...].reshape(2 * count, half), basis_v[turn], preferred_element_type=jnp.float32
-        )
-        odd = lax.broadcasted_iota(jnp.int32, (count, halves.shape[1]), 1) % 2 == 1
-        late = halves[count:]
-        spectra = (halves[:count] + jnp.where(odd, -late, late)).T
-        for b in range(NB // 2):
-            spectrum = spectra[b * rows : (b + 1) * rows]
-            power = jnp.sum(spectrum * spectrum, axis=0, keepdims=True) / BIN
-            white = (spectrum * (keep * lax.rsqrt(power + 1e-05))).astype(jnp.bfloat16)
-            for q in range(groups):
-                send_v[side * (devices // 2) + b * groups + q] = white[:, q * LANES : (q + 1) * LANES]
-        if turn == 0:
-            pl.semaphore_wait(barrier, devices - 1)
-        for plane in far_planes if turn == 0 else near_planes:
-            own = turn == 1 and plane is near_planes[-1]
-            for e in range(pack - 1, 0 if own else -1, -1):
-                remote(plane * pack + flipped(my_place, e)).start()
+        for q in range(groups):
+            if turn == 0:
+                for load in loads[q]:
+                    load.wait()
+            keep = jnp.concatenate(
+                [small_ref[w : w + 1, q * sub_rows : (q + 1) * sub_rows] for w in range(windows)],
+                axis=1,
+            ).astype(jnp.float32)
+            halves = jnp.dot(
+                rec_v[q].reshape(2 * LANES, half), basis_v[turn], preferred_element_type=jnp.float32
+            )
+            late = halves[LANES:]
+            spectra = (halves[:LANES] + jnp.where(odd, -late, late)).T
+            for b in range(NB // 2):
+                spectrum = spectra[b * rows : (b + 1) * rows]
+                power = jnp.sum(spectrum * spectrum, axis=0, keepdims=True) / BIN
+                white = spectrum * (keep * lax.rsqrt(power + 1e-05))
+                send_v[side * (devices // 2) + b * groups + q] = white.astype(jnp.bfloat16)
+            if turn == 0 and q == 0:
+                pl.semaphore_wait(barrier, devices - 1)
+            for plane in far_planes if turn == 0 else near_planes:
+                for v in range(pack // groups - 1, -1, -1):
+                    peer = plane * pack + flipped(my_place // groups, v) * groups + q
+                    if turn == 1 and plane is near_planes[-1] and v == 0:
+                        pl.when(me % groups != q)(remote(peer).start)
+                    else:
+                        remote(peer).start()
     recv_v[me] = send_v[me]
 
     ordered = near_planes[::-1] + far_planes
@@ -152,7 +153,10 @@
             arrival(plane * pack + flipped(my_place, e)).wait_recv()
         if turn == planes - 1:
             for s in range(NSB):
-                own_v[s] = recv_v[small_ref[0, channels + s]]
+                turned = recv_v[small_ref[0, channels + s]].astype(jnp.float32).T * (1.0 / windows)
+                own_v[s] = jnp.concatenate(
+                    [turned[w * sub_rows : (w + 1) * sub_rows] for w in range(windows)], axis=1
+                ).astype(jnp.bfloat16)
             swap = pltpu.make_async_remote_copy(
                 src_ref=own_v, dst_ref=src_ref.at[me % groups],
                 send_sem=src_sem.at[0], recv_sem=src_sem.at[1],
@@ -176,16 +180,13 @@
 
 
 def product_kernel(src_ref, rhs_ref, out_ref, left_v, out_v, out_sem):
-    rows = 2 * BIN
     planes = rhs_ref.shape[1]
-    windows = rhs_ref.shape[2] // rows
     groups, blocks = src_ref.shape[:2]
-    sub_rows = SBLK // groups
     wide = 2
 
-    pieces = [src_ref[q, s] for s in range(blocks) for q in range(groups)]
-    by_window = lanes_to_rows(pieces, sub_rows)
-    left_v[...] = jnp.concatenate(by_window, axis=0).T * (1.0 / windows)
+    left_v[...] = jnp.concatenate(
+        [src_ref[q, s].astype(jnp.float32) for s in range(blocks) for q in range(groups)], axis=0
+    )
 
     def write(place):
         return pltpu.make_async_copy(out_v.at[place], out_ref.at[place], out_sem.at[place])
@@ -235,7 +236,7 @@
         exchange_kernel,
         out_shape=(
             jax.ShapeDtypeStruct((2, planes, depth, LANES), jnp.bfloat16),
-            jax.ShapeDtypeStruct((groups, NSB, rows, LANES), jnp.bfloat16),
+            jax.ShapeDtypeStruct((groups, NSB, sub_rows, depth), jnp.bfloat16),
         ),
         in_specs=[
             pl.BlockSpec(memory_space=pltpu.VMEM),
@@ -245,11 +246,11 @@
         out_specs=(pl.BlockSpec(memory_space=pltpu.VMEM), pl.BlockSpec(memory_space=pltpu.VMEM)),
         scratch_shapes=[
             pltpu.VMEM(basis.shape, jnp.bfloat16),
-            pltpu.VMEM((2, windows * channels, samples // 2), jnp.bfloat16),
+            pltpu.VMEM((groups, 2, LANES, samples // 2), jnp.bfloat16),
             pltpu.VMEM((devices, rows, LANES), jnp.bfloat16),
             pltpu.VMEM((devices, rows, LANES), jnp.bfloat16),
-            pltpu.VMEM((NSB, rows, LANES), jnp.bfloat16),
-            pltpu.SemaphoreType.DMA((2 * groups * windows,)),
+            pltpu.VMEM((NSB, sub_rows, depth), jnp.bfloat16),
+            pltpu.SemaphoreType.DMA((groups, 2 * windows)),
             pltpu.SemaphoreType.DMA((2,)),
             pltpu.SemaphoreType.DMA((devices,)),
             pltpu.SemaphoreType.DMA((devices,)),

time: 18.7 us -> 19 us (1.016)
  Pallas kernels: 17.8 us -> 18.1 us
    pallas_call x1, Pallas kernels: 13.7 us -> 14.1 us  [per_device_kernels(): pl.pallas_call(exchange_kernel, out_shape=(jax.ShapeDtypeStruct((2, plane...]
where the time goes in v6:
time: 19 us; the launch traced here: 18.8 us
  Pallas kernels  18.1 us (95%)
  other arithmetic  0.77 us (4%)
    pallas_call x1, Pallas kernels, per_device_kernels(): pl.pallas_call(exchange_kernel, out_shape=(jax.ShapeDtypeStruct((2, plane...  14.1 us
    pallas_call x1, Pallas kernels, per_device_kernels(): pl.pallas_call(product_kernel, out_shape=jax.ShapeDtypeStruct(out_shape,...  3.98 us
    concatenate x1, other arithmetic, per_device_kernels(): small = jnp.concatenate([quality, padded_ids], axis=1)  0.77 us

profile of v6, /device:TPU:0, one launch (start us, length us, event | category | flops | bytes accessed | tf_op | source)
XLA Modules:
  0.0 18.8 jit_solution(15270013509808091455)
XLA Ops:
  0.0 0.8 %pad_add_fusion.small_ref = s32[4,128]{1,0:T(4,128)S(1)} fusion(s32[1,2]{1,0:T(1,128)} %bitcast.2, s32[4,64]{1,0:T(4,128)} %param.5), kind=kLoop, calls=%fused_computation | loop fusion | flops 512 | bytes 3080 | tf_op jit(solution)/shard_map/concatenate | solution.py:234
  0.8 14.1 %spectra_exchange.1 = (bf16[2,4,256,128]{3,2,1,0:T(8,128)(2,1)S(1)}, bf16[2,2,32,256]{3,2,1,0:T(8,128)(2,1)S(1)}) custom-call(s32[4,128]{1,0:T(4,128)S(1)} %pad_add_fusion.small_ref, bf16[2,1024,256]{2,1,0:T(8,128)(2,1)} %constant.4.clone.basis_ref, bf16[4,64,2048]{2,1,0:T(8,128)(2,1)} %records_ref.1), custom_call_target="tpu_custom_call" | custom-call | tf_op jit(solution)/shard_map/spectra_exchange/pallas_call | solution.py:235
  14.9 4.0 %cross_spectra.1 = bf16[32,128,1024]{2,1,0:T(8,128)(2,1)} custom-call(bf16[2,2,32,256]{3,2,1,0:T(8,128)(2,1)S(1)} %get-tuple-element.7.src_ref, bf16[2,4,256,128]{3,2,1,0:T(8,128)(2,1)S(1)} %get-tuple-element.8.rhs_ref), custom_call_target="tpu_custom_call" | custom-call | tf_op jit(solution)/shard_map/cross_spectra/pallas_call | solution.py:267

commit v7 on v4

--- a/solution.py
+++ b/solution.py
@@ -140,10 +140,18 @@
                 send_v[side * (devices // 2) + b * groups + q] = white[:, q * LANES : (q + 1) * LANES]
         if turn == 0:
             pl.semaphore_wait(barrier, devices - 1)
-        for plane in far_planes if turn == 0 else near_planes:
-            own = turn == 1 and plane is near_planes[-1]
-            for e in range(pack - 1, 0 if own else -1, -1):
-                remote(plane * pack + flipped(my_place, e)).start()
+        if turn == 0:
+            for e in range(pack - 1, -1, -1):
+                for plane in far_planes[: planes // 4]:
+                    remote(plane * pack + flipped(my_place, e)).start()
+    for e in range(pack - 1, -1, -1):
+        for far, near in zip(far_planes[planes // 4 :], near_planes):
+            remote(far * pack + flipped(my_place, e)).start()
+            remote(near * pack + flipped(my_place, e)).start()
+    for near in near_planes[planes // 4 :]:
+        own = near is near_planes[-1]
+        for e in range(pack - 1, 0 if own else -1, -1):
+            remote(near * pack + flipped(my_place, e)).start()
     recv_v[me] = send_v[me]
 
     ordered = near_planes[::-1] + far_planes
@@ -152,7 +160,10 @@
             arrival(plane * pack + flipped(my_place, e)).wait_recv()
         if turn == planes - 1:
             for s in range(NSB):
-                own_v[s] = recv_v[small_ref[0, channels + s]]
+                turned = recv_v[small_ref[0, channels + s]].astype(jnp.float32).T * (1.0 / windows)
+                own_v[s] = jnp.concatenate(
+                    [turned[w * sub_rows : (w + 1) * sub_rows] for w in range(windows)], axis=1
+                ).astype(jnp.bfloat16)
             swap = pltpu.make_async_remote_copy(
                 src_ref=own_v, dst_ref=src_ref.at[me % groups],
                 send_sem=src_sem.at[0], recv_sem=src_sem.at[1],
@@ -176,16 +187,13 @@
 
 
 def product_kernel(src_ref, rhs_ref, out_ref, left_v, out_v, out_sem):
-    rows = 2 * BIN
     planes = rhs_ref.shape[1]
-    windows = rhs_ref.shape[2] // rows
     groups, blocks = src_ref.shape[:2]
-    sub_rows = SBLK // groups
     wide = 2
 
-    pieces = [src_ref[q, s] for s in range(blocks) for q in range(groups)]
-    by_window = lanes_to_rows(pieces, sub_rows)
-    left_v[...] = jnp.concatenate(by_window, axis=0).T * (1.0 / windows)
+    left_v[...] = jnp.concatenate(
+        [src_ref[q, s].astype(jnp.float32) for s in range(blocks) for q in range(groups)], axis=0
+    )
 
     def write(place):
         return pltpu.make_async_copy(out_v.at[place], out_ref.at[place], out_sem.at[place])
@@ -235,7 +243,7 @@
         exchange_kernel,
         out_shape=(
             jax.ShapeDtypeStruct((2, planes, depth, LANES), jnp.bfloat16),
-            jax.ShapeDtypeStruct((groups, NSB, rows, LANES), jnp.bfloat16),
+            jax.ShapeDtypeStruct((groups, NSB, sub_rows, depth), jnp.bfloat16),
         ),
         in_specs=[
             pl.BlockSpec(memory_space=pltpu.VMEM),
@@ -248,7 +256,7 @@
             pltpu.VMEM((2, windows * channels, samples // 2), jnp.bfloat16),
             pltpu.VMEM((devices, rows, LANES), jnp.bfloat16),
             pltpu.VMEM((devices, rows, LANES), jnp.bfloat16),
-            pltpu.VMEM((NSB, rows, LANES), jnp.bfloat16),
+            pltpu.VMEM((NSB, sub_rows, depth), jnp.bfloat16),
             pltpu.SemaphoreType.DMA((2 * groups * windows,)),
             pltpu.SemaphoreType.DMA((2,)),
             pltpu.SemaphoreType.DMA((devices,)),

time: 18.7 us -> 18.6 us (level)
  no operation moved by 1% of the time
where the time goes in v7:
time: 18.6 us; the launch traced here: 18.4 us
  Pallas kernels  17.7 us (95%)
  other arithmetic  0.77 us (4%)
    pallas_call x1, Pallas kernels, per_device_kernels(): pl.pallas_call(exchange_kernel, out_shape=(jax.ShapeDtypeStruct((2, plane...  13.7 us
    pallas_call x1, Pallas kernels, per_device_kernels(): pl.pallas_call(product_kernel, out_shape=jax.ShapeDtypeStruct(out_shape,...  3.98 us
    concatenate x1, other arithmetic, per_device_kernels(): small = jnp.concatenate([quality, padded_ids], axis=1)  0.77 us

profile of v7, /device:TPU:0, one launch (start us, length us, event | category | flops | bytes accessed | tf_op | source)
XLA Modules:
  0.0 18.4 jit_solution(6747670032533200966)
XLA Ops:
  0.0 0.8 %pad_add_fusion.small_ref = s32[4,128]{1,0:T(4,128)S(1)} fusion(s32[1,2]{1,0:T(1,128)} %bitcast.2, s32[4,64]{1,0:T(4,128)} %param.5), kind=kLoop, calls=%fused_computation | loop fusion | flops 512 | bytes 3080 | tf_op jit(solution)/shard_map/concatenate | solution.py:241
  0.8 13.7 %spectra_exchange.1 = (bf16[2,4,256,128]{3,2,1,0:T(8,128)(2,1)S(1)}, bf16[2,2,32,256]{3,2,1,0:T(8,128)(2,1)S(1)}) custom-call(s32[4,128]{1,0:T(4,128)S(1)} %pad_add_fusion.small_ref, bf16[2,1024,256]{2,1,0:T(8,128)(2,1)} %constant.4.clone.basis_ref, bf16[4,64,2048]{2,1,0:T(8,128)(2,1)} %records_ref.1), custom_call_target="tpu_custom_call" | custom-call | tf_op jit(solution)/shard_map/spectra_exchange/pallas_call | solution.py:242
  14.5 4.0 %cross_spectra.1 = bf16[32,128,1024]{2,1,0:T(8,128)(2,1)} custom-call(bf16[2,2,32,256]{3,2,1,0:T(8,128)(2,1)S(1)} %get-tuple-element.7.src_ref, bf16[2,4,256,128]{3,2,1,0:T(8,128)(2,1)S(1)} %get-tuple-element.8.rhs_ref), custom_call_target="tpu_custom_call" | custom-call | tf_op jit(solution)/shard_map/cross_spectra/pallas_call | solution.py:274

commit v8 on v7

--- a/solution.py
+++ b/solution.py
@@ -123,6 +123,15 @@
     far_planes = [
         near_side * u + (1 - near_side) * (planes - 1 - u) for u in range(planes // 2)
     ]
+    outer_near = [
+        near_side * (planes - 1 - u) + (1 - near_side) * u for u in range(planes // 2)
+    ]
+
+    def send_plane(plane):
+        for e in range(pack - 1, 0, -1):
+            remote(plane * pack + flipped(my_place, e)).start()
+        pl.when(plane != my_plane)(remote(plane * pack + my_place).start)
+
     near_planes = [flipped(my_plane, u) for u in range(planes // 2 - 1, -1, -1)]
     for turn, side in enumerate(sides):
         basis_loads[turn].wait()
@@ -141,17 +150,11 @@
         if turn == 0:
             pl.semaphore_wait(barrier, devices - 1)
         if turn == 0:
-            for e in range(pack - 1, -1, -1):
-                for plane in far_planes[: planes // 4]:
-                    remote(plane * pack + flipped(my_place, e)).start()
-    for e in range(pack - 1, -1, -1):
-        for far, near in zip(far_planes[planes // 4 :], near_planes):
-            remote(far * pack + flipped(my_place, e)).start()
-            remote(near * pack + flipped(my_place, e)).start()
-    for near in near_planes[planes // 4 :]:
-        own = near is near_planes[-1]
-        for e in range(pack - 1, 0 if own else -1, -1):
-            remote(near * pack + flipped(my_place, e)).start()
+            send_plane(far_planes[0])
+    for u in range(planes // 2):
+        if u:
+            send_plane(far_planes[u])
+        send_plane(outer_near[u])
     recv_v[me] = send_v[me]
 
     ordered = near_planes[::-1] + far_planes

time: 18.6 us -> 18.8 us (1.011)
  no operation moved by 1% of the time
where the time goes in v8:
time: 18.8 us; the launch traced here: 18.6 us
  Pallas kernels  17.8 us (95%)
  other arithmetic  0.77 us (4%)
    pallas_call x1, Pallas kernels, per_device_kernels(): pl.pallas_call(exchange_kernel, out_shape=(jax.ShapeDtypeStruct((2, plane...  13.9 us
    pallas_call x1, Pallas kernels, per_device_kernels(): pl.pallas_call(product_kernel, out_shape=jax.ShapeDtypeStruct(out_shape,...  3.98 us
    concatenate x1, other arithmetic, per_device_kernels(): small = jnp.concatenate([quality, padded_ids], axis=1)  0.77 us

profile of v8, /device:TPU:0, one launch (start us, length us, event | category | flops | bytes accessed | tf_op | source)
XLA Modules:
  0.0 18.6 jit_solution(6327687738455335777)
XLA Ops:
  0.0 0.8 %pad_add_fusion.small_ref = s32[4,128]{1,0:T(4,128)S(1)} fusion(s32[1,2]{1,0:T(1,128)} %bitcast.2, s32[4,64]{1,0:T(4,128)} %param.5), kind=kLoop, calls=%fused_computation | loop fusion | flops 512 | bytes 3080 | tf_op jit(solution)/shard_map/concatenate | solution.py:244
  0.8 13.9 %spectra_exchange.1 = (bf16[2,4,256,128]{3,2,1,0:T(8,128)(2,1)S(1)}, bf16[2,2,32,256]{3,2,1,0:T(8,128)(2,1)S(1)}) custom-call(s32[4,128]{1,0:T(4,128)S(1)} %pad_add_fusion.small_ref, bf16[2,1024,256]{2,1,0:T(8,128)(2,1)} %constant.4.clone.basis_ref, bf16[4,64,2048]{2,1,0:T(8,128)(2,1)} %records_ref.1), custom_call_target="tpu_custom_call" | custom-call | tf_op jit(solution)/shard_map/spectra_exchange/pallas_call | solution.py:245
  14.6 4.0 %cross_spectra.1 = bf16[32,128,1024]{2,1,0:T(8,128)(2,1)} custom-call(bf16[2,2,32,256]{3,2,1,0:T(8,128)(2,1)S(1)} %get-tuple-element.7.src_ref, bf16[2,4,256,128]{3,2,1,0:T(8,128)(2,1)S(1)} %get-tuple-element.8.rhs_ref), custom_call_target="tpu_custom_call" | custom-call | tf_op jit(solution)/shard_map/cross_spectra/pallas_call | solution.py:277

commit v9 on v8

--- a/solution.py
+++ b/solution.py
@@ -153,6 +153,8 @@
             send_plane(far_planes[0])
     for u in range(planes // 2):
         if u:
+            for e in range(pack):
+                remote(far_planes[u - 1] * pack + e).wait_send()
             send_plane(far_planes[u])
         send_plane(outer_near[u])
     recv_v[me] = send_v[me]
@@ -181,12 +183,14 @@
             rhs_ref[0, plane, w * rows + BIN : (w + 1) * rows] = imag.astype(jnp.bfloat16)
             rhs_ref[1, plane, w * rows : w * rows + BIN] = imag.astype(jnp.bfloat16)
             rhs_ref[1, plane, w * rows + BIN : (w + 1) * rows] = (-real).astype(jnp.bfloat16)
-    for off in range(1, devices):
+    for off in range(1, devices // 2):
         remote(flipped(me, off)).wait_send()
+    for e in range(pack):
+        remote(far_planes[-1] * pack + e).wait_send()
     swap.wait()
 
 
-STEP_BINS = 4
+STEP_BINS = 2
 
 
 def product_kernel(src_ref, rhs_ref, out_ref, left_v, out_v, out_sem):

time: 18.8 us -> 18.6 us (0.989)
  no operation moved by 1% of the time
where the time goes in v9:
time: 18.6 us; the launch traced here: 18.5 us
  Pallas kernels  17.7 us (95%)
  other arithmetic  0.77 us (4%)
    pallas_call x1, Pallas kernels, per_device_kernels(): pl.pallas_call(exchange_kernel, out_shape=(jax.ShapeDtypeStruct((2, plane...  13.9 us
    pallas_call x1, Pallas kernels, per_device_kernels(): pl.pallas_call(product_kernel, out_shape=jax.ShapeDtypeStruct(out_shape,...  3.84 us
    concatenate x1, other arithmetic, per_device_kernels(): small = jnp.concatenate([quality, padded_ids], axis=1)  0.77 us

profile of v9, /device:TPU:0, one launch (start us, length us, event | category | flops | bytes accessed | tf_op | source)
XLA Modules:
  0.0 18.5 jit_solution(8448926400491403471)
XLA Ops:
  0.0 0.8 %pad_add_fusion.small_ref = s32[4,128]{1,0:T(4,128)S(1)} fusion(s32[1,2]{1,0:T(1,128)} %bitcast.2, s32[4,64]{1,0:T(4,128)} %param.5), kind=kLoop, calls=%fused_computation | loop fusion | flops 512 | bytes 3080 | tf_op jit(solution)/shard_map/concatenate | solution.py:248
  0.8 13.9 %spectra_exchange.1 = (bf16[2,4,256,128]{3,2,1,0:T(8,128)(2,1)S(1)}, bf16[2,2,32,256]{3,2,1,0:T(8,128)(2,1)S(1)}) custom-call(s32[4,128]{1,0:T(4,128)S(1)} %pad_add_fusion.small_ref, bf16[2,1024,256]{2,1,0:T(8,128)(2,1)} %constant.4.clone.basis_ref, bf16[4,64,2048]{2,1,0:T(8,128)(2,1)} %records_ref.1), custom_call_target="tpu_custom_call" | custom-call | tf_op jit(solution)/shard_map/spectra_exchange/pallas_call | solution.py:249
  14.6 3.8 %cross_spectra.1 = bf16[32,128,1024]{2,1,0:T(8,128)(2,1)} custom-call(bf16[2,2,32,256]{3,2,1,0:T(8,128)(2,1)S(1)} %get-tuple-element.7.src_ref, bf16[2,4,256,128]{3,2,1,0:T(8,128)(2,1)S(1)} %get-tuple-element.8.rhs_ref), custom_call_target="tpu_custom_call" | custom-call | tf_op jit(solution)/shard_map/cross_spectra/pallas_call | solution.py:281

commit v10 on v6

--- a/solution.py
+++ b/solution.py
@@ -138,13 +138,17 @@
                 send_v[side * (devices // 2) + b * groups + q] = white.astype(jnp.bfloat16)
             if turn == 0 and q == 0:
                 pl.semaphore_wait(barrier, devices - 1)
-            for plane in far_planes if turn == 0 else near_planes:
+            for plane in far_planes[:1] if turn == 0 else near_planes:
                 for v in range(pack // groups - 1, -1, -1):
                     peer = plane * pack + flipped(my_place // groups, v) * groups + q
                     if turn == 1 and plane is near_planes[-1] and v == 0:
                         pl.when(me % groups != q)(remote(peer).start)
                     else:
                         remote(peer).start()
+        if turn == 0:
+            for plane in far_planes[1:]:
+                for e in range(pack - 1, -1, -1):
+                    remote(plane * pack + flipped(my_place, e)).start()
     recv_v[me] = send_v[me]
 
     ordered = near_planes[::-1] + far_planes
@@ -176,7 +180,7 @@
     swap.wait()
 
 
-STEP_BINS = 4
+STEP_BINS = 2
 
 
 def product_kernel(src_ref, rhs_ref, out_ref, left_v, out_v, out_sem):

time: 19 us -> 18.5 us (0.974)
  Pallas kernels: 18.1 us -> 17.6 us
    pallas_call x1, Pallas kernels: 14.1 us -> 13.7 us  [per_device_kernels(): pl.pallas_call(exchange_kernel, out_shape=(jax.ShapeDtypeStruct((2, plane...]
where the time goes in v10:
time: 18.5 us; the launch traced here: 18.3 us
  Pallas kernels  17.6 us (95%)
  other arithmetic  0.77 us (4%)
    pallas_call x1, Pallas kernels, per_device_kernels(): pl.pallas_call(exchange_kernel, out_shape=(jax.ShapeDtypeStruct((2, plane...  13.7 us
    pallas_call x1, Pallas kernels, per_device_kernels(): pl.pallas_call(product_kernel, out_shape=jax.ShapeDtypeStruct(out_shape,...  3.84 us
    concatenate x1, other arithmetic, per_device_kernels(): small = jnp.concatenate([quality, padded_ids], axis=1)  0.77 us

profile of v10, /device:TPU:0, one launch (start us, length us, event | category | flops | bytes accessed | tf_op | source)
XLA Modules:
  0.0 18.3 jit_solution(11721541600368496373)
XLA Ops:
  0.0 0.8 %pad_add_fusion.small_ref = s32[4,128]{1,0:T(4,128)S(1)} fusion(s32[1,2]{1,0:T(1,128)} %bitcast.2, s32[4,64]{1,0:T(4,128)} %param.5), kind=kLoop, calls=%fused_computation | loop fusion | flops 512 | bytes 3080 | tf_op jit(solution)/shard_map/concatenate | solution.py:238
  0.8 13.7 %spectra_exchange.1 = (bf16[2,4,256,128]{3,2,1,0:T(8,128)(2,1)S(1)}, bf16[2,2,32,256]{3,2,1,0:T(8,128)(2,1)S(1)}) custom-call(s32[4,128]{1,0:T(4,128)S(1)} %pad_add_fusion.small_ref, bf16[2,1024,256]{2,1,0:T(8,128)(2,1)} %constant.4.clone.basis_ref, bf16[4,64,2048]{2,1,0:T(8,128)(2,1)} %records_ref.1), custom_call_target="tpu_custom_call" | custom-call | tf_op jit(solution)/shard_map/spectra_exchange/pallas_call | solution.py:239
  14.5 3.8 %cross_spectra.1 = bf16[32,128,1024]{2,1,0:T(8,128)(2,1)} custom-call(bf16[2,2,32,256]{3,2,1,0:T(8,128)(2,1)S(1)} %get-tuple-element.7.src_ref, bf16[2,4,256,128]{3,2,1,0:T(8,128)(2,1)S(1)} %get-tuple-element.8.rhs_ref), custom_call_target="tpu_custom_call" | custom-call | tf_op jit(solution)/shard_map/cross_spectra/pallas_call | solution.py:271
